TPU v7x, 512 devices: a whole 4x4x16 slice. The times are simulated.
512 devices in a mesh: frame: 64 (over x, z), uly: 8 (over y, core).
Axes of the slice: x: 4, y: 4, z: 16, core: 2. Of those that a mesh axis runs over, the one named last changes fastest.
Arguments:
- queries: bfloat16 [65536, 3072], P(('frame', 'uly')), may hold values from -7.5 to 7.5
- keys: bfloat16 [65536, 3072], P(('frame', 'uly')), may hold values from -7.5 to 7.5
- values: bfloat16 [65536, 3072], P(('frame', 'uly')), may hold values from -6 to 6
- text_k: bfloat16 [4, 128, 3072], P(None, 'frame', 'uly'), may hold values from -7.5 to 7.5
- text_v: bfloat16 [4, 128, 3072], P(None, 'frame', 'uly'), may hold values from -6 to 6
- text_len: int32 [4], replicated, may hold values from 1 to 128, 256 in all
- seg_frames: int32 [4], replicated, may hold values from 1 to 512, 1024 in all
Outputs:
- grad_queries: bfloat16 [65536, 3072], P(('frame', 'uly'))
- grad_keys: bfloat16 [65536, 3072], P(('frame', 'uly'))
- grad_values: bfloat16 [65536, 3072], P(('frame', 'uly'))
- grad_text_k: float32 [4, 128, 3072], P(None, 'frame', 'uly')
- grad_text_v: float32 [4, 128, 3072], P(None, 'frame', 'uly')
Inputs may be any that keep to these rules, and one draw needn't show every extreme that they name: `text_len`: the entries sum to 256. `seg_frames`: the segments cover the 1024 frames in order and sum to 1024.
All inputs are finite; a program needn't handle non-finite values.
Results may differ from a plain program's by a relative error of at most 0.015.
Values may be sent and summed in bfloat16 or wider, within the bound.
A program may use at most 128 MiB of HBM per device.

v0:
```python
import jax
import jax.numpy as jnp
from jax import lax
from jax.sharding import PartitionSpec as P

HD = 128
FT = 64
FR_GRP = 16
TXT = 128
NSEG = 4


def padded_2(block, sides, width):
    for axis, dim in sides:
        count = lax.axis_size(axis)
        forward = [(i, i + 1) for i in range(count - 1)]
        backward = [(target, source) for source, target in forward]
        low = lax.ppermute(
            lax.slice_in_dim(block, block.shape[dim] - width, None, axis=dim), axis, forward
        )
        high = lax.ppermute(lax.slice_in_dim(block, 0, width, axis=dim), axis, backward)
        block = jnp.concatenate([low, block, high], axis=dim)
    return block


def normalize(scores):
    top = jnp.max(scores, axis=-1, keepdims=True)
    total = jnp.log(jnp.sum(jnp.exp(scores - top), axis=-1, keepdims=True))
    return jnp.exp(scores - (top + total))


def attend(queries, keys, values, allowed):
    scores = jnp.einsum("qhd,khd->hqk", queries, keys, preferred_element_type=jnp.float32) * HD ** (
        -0.5
    )
    scores = jnp.where(allowed[None], scores, -jnp.inf)
    probs = normalize(scores)
    rounded = probs.astype(jnp.bfloat16)
    attended = jnp.einsum("hqk,khd->qhd", rounded, values, preferred_element_type=jnp.float32)
    return (probs, rounded, attended)


def attend_back(probs, rounded, attended, grad, queries, keys, values):
    scale = HD ** (-0.5)
    delta = jnp.sum(grad.astype(jnp.float32) * attended, axis=-1).T
    dprob = jnp.einsum("qhd,khd->hqk", grad, values, preferred_element_type=jnp.float32)
    dscore = (probs * (dprob - delta[:, :, None])).astype(jnp.bfloat16)
    grad_q = scale * jnp.einsum("hqk,khd->qhd", dscore, keys, preferred_element_type=jnp.float32)
    grad_k = scale * jnp.einsum("hqk,qhd->khd", dscore, queries, preferred_element_type=jnp.float32)
    grad_v = jnp.einsum("hqk,qhd->khd", rounded, grad, preferred_element_type=jnp.float32)
    return (grad_q, grad_k, grad_v)


def window_mask(query_frames, key_frames, frame_count):
    near = jnp.abs(query_frames[:, None] - key_frames[None, :]) <= 1
    inside = (key_frames >= 0) & (key_frames < frame_count)
    return near & inside[None, :]


def body(queries, keys, values, text_k, text_v, text_len, seg_frames):
    frame_count = FR_GRP * lax.axis_size("frame")
    first = lax.axis_index("frame") * FR_GRP
    head_q, head_k, head_v = (
        lax.all_to_all(queries, "uly", split_axis=1, concat_axis=0, tiled=True),
        lax.all_to_all(keys, "uly", split_axis=1, concat_axis=0, tiled=True),
        lax.all_to_all(values, "uly", split_axis=1, concat_axis=0, tiled=True),
    )
    rows, width = head_q.shape
    heads = width // HD
    prompt_k, prompt_v = (
        lax.all_gather(text_k, "frame", axis=1, tiled=True),
        lax.all_gather(text_v, "frame", axis=1, tiled=True),
    )
    bounds = jnp.cumsum(seg_frames)
    own_frames = first + jnp.arange(FR_GRP, dtype=jnp.int32)
    segment = jnp.sum((own_frames[:, None] >= bounds[None, :]).astype(jnp.int32), axis=1)
    picks = segment[:, None] == jnp.arange(NSEG, dtype=jnp.int32)[None, :]
    frame_len = jnp.sum(jnp.where(picks, text_len[None, :], 0), axis=1)
    frame_tk = jnp.einsum(
        "fs,stc->ftc", picks.astype(jnp.bfloat16), prompt_k, preferred_element_type=jnp.float32
    ).astype(jnp.bfloat16)
    frame_tv = jnp.einsum(
        "fs,stc->ftc", picks.astype(jnp.bfloat16), prompt_v, preferred_element_type=jnp.float32
    ).astype(jnp.bfloat16)
    kv_pair = jnp.stack([head_k, head_v])
    depth = 1
    padded = padded_2(kv_pair, (("frame", 1),), FT)
    ext_rows = padded.shape[1]
    ext_k = padded[0].reshape(ext_rows, heads, HD)
    ext_v = padded[1].reshape(ext_rows, heads, HD)
    ext_frames = first - depth + jnp.arange(ext_rows, dtype=jnp.int32) // FT
    q_heads = head_q.reshape(rows, heads, HD)
    acc_k = jnp.zeros((ext_rows, heads, HD), jnp.float32)
    acc_v = jnp.zeros((ext_rows, heads, HD), jnp.float32)
    text_gk = jnp.zeros((NSEG, TXT, heads, HD), jnp.float32)
    text_gv = jnp.zeros((NSEG, TXT, heads, HD), jnp.float32)
    dq_parts = []
    grad_parts = []
    for block in range(FR_GRP // 2):
        start = block * 2 * FT
        q_blk = q_heads[start : start + 2 * FT]
        k_start = (depth - 1 + 2 * block) * FT
        k_blk = ext_k[k_start : k_start + 4 * FT]
        v_blk = ext_v[k_start : k_start + 4 * FT]
        q_frames = first + 2 * block + jnp.arange(2 * FT, dtype=jnp.int32) // FT
        allowed = window_mask(q_frames, ext_frames[k_start : k_start + 4 * FT], frame_count)
        probs, rounded, self_out = attend(q_blk, k_blk, v_blk, allowed)
        q_pair = q_blk.reshape(2, FT, heads, HD)
        tk_pair = frame_tk[2 * block : 2 * block + 2].reshape(2, TXT, heads, HD)
        tv_pair = frame_tv[2 * block : 2 * block + 2].reshape(2, TXT, heads, HD)
        len_pair = frame_len[2 * block : 2 * block + 2]
        text_used = jnp.arange(TXT, dtype=jnp.int32)[None, None, :] < len_pair[:, None, None]
        c_probs, c_rounded, cross_out = jax.vmap(attend)(q_pair, tk_pair, tv_pair, text_used)
        grad = (self_out + cross_out.reshape(2 * FT, heads, HD)).astype(jnp.bfloat16)
        dq_self, dk_blk, dv_blk = attend_back(probs, rounded, self_out, grad, q_blk, k_blk, v_blk)
        dq_cross, dtk_pair, dtv_pair = jax.vmap(attend_back)(
            c_probs, c_rounded, cross_out, grad.reshape(2, FT, heads, HD), q_pair, tk_pair, tv_pair
        )
        dq_parts.append((dq_self + dq_cross.reshape(2 * FT, heads, HD)).astype(jnp.bfloat16))
        grad_parts.append(grad)
        acc_k = acc_k.at[k_start : k_start + 4 * FT].add(dk_blk)
        acc_v = acc_v.at[k_start : k_start + 4 * FT].add(dv_blk)
        onehot = picks[2 * block : 2 * block + 2].astype(jnp.float32)[:, :, None, None, None]
        text_gk = text_gk + jnp.sum(onehot * dtk_pair[:, None], axis=0)
        text_gv = text_gv + jnp.sum(onehot * dtv_pair[:, None], axis=0)
    edges = jnp.stack(
        [jnp.concatenate([acc_k[:FT], acc_k[-FT:]]), jnp.concatenate([acc_v[:FT], acc_v[-FT:]])]
    ).reshape(2, 2 * FT, width)
    returned = padded_2(edges.astype(jnp.bfloat16), (("frame", 1),), FT).astype(edges.dtype)
    own_k = acc_k[FT : FT + rows].reshape(rows, width)
    own_v = acc_v[FT : FT + rows].reshape(rows, width)
    own_k = own_k.at[:FT].add(returned[0, :FT]).at[rows - FT :].add(returned[0, -FT:])
    own_v = own_v.at[:FT].add(returned[1, :FT]).at[rows - FT :].add(returned[1, -FT:])
    dq_heads = jnp.concatenate(dq_parts).reshape(rows, width)
    out_q, out_k, out_v = (
        lax.all_to_all(dq_heads, "uly", split_axis=0, concat_axis=1, tiled=True),
        lax.all_to_all(own_k.astype(jnp.bfloat16), "uly", split_axis=0, concat_axis=1, tiled=True),
        lax.all_to_all(own_v.astype(jnp.bfloat16), "uly", split_axis=0, concat_axis=1, tiled=True),
    )
    sum_k, sum_v = (
        lax.psum_scatter(
            text_gk.reshape(NSEG, TXT, width), "frame", scatter_dimension=1, tiled=True
        ),
        lax.psum_scatter(
            text_gv.reshape(NSEG, TXT, width), "frame", scatter_dimension=1, tiled=True
        ),
    )
    return (out_q, out_k, out_v, sum_k, sum_v)


def solution(mesh):
    placed = (
        P(("frame", "uly"), None),
        P(("frame", "uly"), None),
        P(("frame", "uly"), None),
        P(None, "frame", "uly"),
        P(None, "frame", "uly"),
        P(),
        P(),
    )
    return jax.shard_map(
        body,
        mesh=mesh,
        in_specs=placed,
        out_specs=(
            P(("frame", "uly"), None),
            P(("frame", "uly"), None),
            P(("frame", "uly"), None),
            P(None, "frame", "uly"),
            P(None, "frame", "uly"),
        ),
        check_vma=False,
    )
```

profile of v0, /device:TPU:24, one launch (start us, length us, event | category | flops | bytes accessed | tf_op | source)
XLA Modules:
  0.0 769.7 jit_solution(17636345466514365449)
XLA Ops:
  7.2 2.3 copy.1011
  9.5 9.1 %all-to-all-start.2 = ((bf16[128,8,384]{0,2,1:T(8,128)(2,1)}), bf16[128,8,384]{0,2,1:T(8,128)(2,1)S(1)}, u32[]{:S(2)}, u32[]{:S(2)}) async-start(bf16[128,8,384]{0,2,1:T(8,128)(2,1)} %bitcast.7), calls=%async_computation.2 | async-start | bytes 1572864 | tf_op jit(solution)/shard_map/all_to_all | solution.py:64
  19.8 96.9 %all_gather.7 = bf16[4,128,384]{2,0,1:T(4,128)(2,1)S(1)} all-gather(bf16[4,2,384]{2,0,1:T(4,128)(2,1)S(1)} %copy.1019), channel_id=1, replica_groups=mesh['frame'=64,'uly'=8] {'frame'}, dimensions={1}, use_global_device_ids=true | all-gather | bytes 399360 | tf_op jit(solution)/shard_map/all_gather | solution.py:71
  119.6 92.7 %all_gather.6 = bf16[4,128,384]{2,0,1:T(4,128)(2,1)S(1)} all-gather(bf16[4,2,384]{2,0,1:T(4,128)(2,1)S(1)} %copy.1017), channel_id=1, replica_groups=mesh['frame'=64,'uly'=8] {'frame'}, dimensions={1}, use_global_device_ids=true | all-gather | bytes 399360 | tf_op jit(solution)/shard_map/all_gather | solution.py:72
  213.1 2.3 copy.1008
  222.9 2.2 fusion.233
  225.2 4.9 all-to-all-start.1
  231.8 2.3 copy.1006
  258.8 4.8 all-to-all-start
  267.2 7.5 all-to-all-done
  278.2 5.5 collective-permute-start
  314.3 2.0 pad_maximum_fusion.3
  406.5 2.1 fusion.132
  428.4 2.3 copy.1213
  433.0 6.2 all-to-all-start.3
  447.0 5.2 collective-permute-start.2
  484.5 2.3 copy.1262
  491.6 2.0 scatter-add.94
  498.6 4.8 all-to-all-start.4
  505.5 9.0 %all-to-all-done.4 = bf16[8,128,384]{1,2,0:T(8,128)(2,1)S(1)} async-done(((bf16[8,128,384]{1,2,0:T(8,128)(2,1)}), bf16[8,128,384]{1,2,0:T(8,128)(2,1)S(1)}, u32[]{:S(2)}, u32[]{:S(2)}) %all-to-all-start.4) | async-done | bytes 786464 | tf_op jit(solution)/shard_map/all_to_all | solution.py:137
  514.5 5.6 all-to-all-start.5
  522.0 2.3 copy.1281
  525.4 5.7 all-to-all-done.5
  532.3 227.6 %all-reduce.7.cloned.1.call-done = (f32[4,128,384]{2,0,1:T(4,128)}, f32[4,128,384]{2,0,1:T(4,128)}) async-done(((f32[4,128,384]{2,0,1:T(4,128)}, f32[4,128,384]{2,0,1:T(4,128)}), (f32[4,128,384]{2,0,1:T(4,128)}, f32[4,128,384]{2,0,1:T(4,128)})) %all-reduce.7.cloned.1.call-update) | async-done | bytes 1572880
  (758 shorter events, 244.2 us)
Async XLA Ops:
  7.2 109.5 %copy-start.213 = (s32[4]{0:T(128)S(1)}, s32[4]{0:T(128)}, u32[]{:S(2)}) copy-start(s32[4]{0:T(128)} %param.53) | copy-start | bytes 52
  9.5 215.7 %all-to-all-start.2 = ((bf16[128,8,384]{0,2,1:T(8,128)(2,1)}), bf16[128,8,384]{0,2,1:T(8,128)(2,1)S(1)}, u32[]{:S(2)}, u32[]{:S(2)}) async-start(bf16[128,8,384]{0,2,1:T(8,128)(2,1)} %bitcast.7), calls=%async_computation.2 | async-start | bytes 1572864 | tf_op jit(solution)/shard_map/all_to_all | solution.py:64
  119.5 93.4 %copy-start.214 = (s32[4]{0:T(128)S(1)}, s32[4]{0:T(128)}, u32[]{:S(2)}) copy-start(s32[4]{0:T(128)} %param.52) | copy-start | bytes 52
  225.2 33.6 %all-to-all-start.1 = ((bf16[128,8,384]{0,2,1:T(8,128)(2,1)}), bf16[128,8,384]{0,2,1:T(8,128)(2,1)S(1)}, u32[]{:S(2)}, u32[]{:S(2)}) async-start(bf16[128,8,384]{0,2,1:T(8,128)(2,1)} %bitcast.3), calls=%async_computation.1 | async-start | bytes 1572864 | tf_op jit(solution)/shard_map/all_to_all | solution.py:66
  230.9 34.9 %copy-start.36 = (bf16[2,128,384]{1,2,0:T(8,128)(2,1)}, bf16[2,128,384]{1,2,0:T(8,128)(2,1)S(1)}, u32[]{:S(2)}) copy-start(bf16[2,128,384]{1,2,0:T(8,128)(2,1)S(1)} %copy.1020) | copy-start | bytes 589828
  234.3 49.7 %copy-start.34 = (bf16[2,128,384]{1,2,0:T(8,128)(2,1)}, bf16[2,128,384]{1,2,0:T(8,128)(2,1)S(1)}, u32[]{:S(2)}) copy-start(bf16[2,128,384]{1,2,0:T(8,128)(2,1)S(1)} %copy.1043) | copy-start | bytes 589828
  235.4 49.4 %copy-start.38 = (bf16[2,128,384]{1,2,0:T(8,128)(2,1)}, bf16[2,128,384]{1,2,0:T(8,128)(2,1)S(1)}, u32[]{:S(2)}) copy-start(bf16[2,128,384]{1,2,0:T(8,128)(2,1)S(1)} %copy.1068) | copy-start | bytes 589828
  236.5 49.2 %copy-start.40 = (bf16[2,128,384]{1,2,0:T(8,128)(2,1)}, bf16[2,128,384]{1,2,0:T(8,128)(2,1)S(1)}, u32[]{:S(2)}) copy-start(bf16[2,128,384]{1,2,0:T(8,128)(2,1)S(1)} %copy.1093) | copy-start | bytes 589828
  238.6 48.0 %copy-start.42 = (bf16[2,128,384]{1,2,0:T(8,128)(2,1)}, bf16[2,128,384]{1,2,0:T(8,128)(2,1)S(1)}, u32[]{:S(2)}) copy-start(bf16[2,128,384]{1,2,0:T(8,128)(2,1)S(1)} %copy.1118) | copy-start | bytes 589828
  258.8 15.9 %all-to-all-start = ((bf16[128,8,384]{0,2,1:T(8,128)(2,1)}), bf16[128,8,384]{0,2,1:T(8,128)(2,1)S(1)}, u32[]{:S(2)}, u32[]{:S(2)}) async-start(bf16[128,8,384]{0,2,1:T(8,128)(2,1)} %bitcast), calls=%async_computation | async-start | bytes 1572864 | tf_op jit(solution)/shard_map/all_to_all | solution.py:65
  267.0 33.8 %copy-start.7 = (f32[2,3,64,128]{3,2,1,0:T(8,128)}, f32[2,3,64,128]{3,2,1,0:T(8,128)S(1)}, u32[]{:S(2)}) copy-start(f32[2,3,64,128]{3,2,1,0:T(8,128)S(1)} %get-tuple-element.382) | copy-start | bytes 589828
  276.7 37.6 %collective-permute-start.1 = (bf16[2,64,384]{2,1,0:T(8,128)(2,1)}, bf16[2,64,384]{2,1,0:T(8,128)(2,1)}, u32[]{:S(2)}, u32[]{:S(2)}) collective-permute-start(bf16[2,64,384]{2,1,0:T(8,128)(2,1)} %get-tuple-element.305), channel_id=1, source_target_pairs={{8,0},{16,8},{24,16},{32,24},{40,32},{48,40},{56,48},{64,56},{72,6... | collective-permute-start | bytes 294920 | tf_op jit(solution)/shard_map/ppermute | solution.py:21
  278.2 36.1 %collective-permute-start = (bf16[2,64,384]{2,1,0:T(8,128)(2,1)}, bf16[2,64,384]{2,1,0:T(8,128)(2,1)}, u32[]{:S(2)}, u32[]{:S(2)}) collective-permute-start(bf16[2,64,384]{2,1,0:T(8,128)(2,1)} %get-tuple-element.306), channel_id=1, source_target_pairs={{0,8},{8,16},{16,24},{24,32},{32,40},{40,48},{48,56},{56,64},{64,7... | collective-permute-start | bytes 294920 | tf_op jit(solution)/shard_map/ppermute | solution.py:18
  284.3 17.8 %copy-start.9 = (f32[2,3,64,128]{3,2,1,0:T(8,128)}, f32[2,3,64,128]{3,2,1,0:T(8,128)S(1)}, u32[]{:S(2)}) copy-start(f32[2,3,64,128]{3,2,1,0:T(8,128)S(1)} %get-tuple-element.386) | copy-start | bytes 589828
  285.1 17.2 %copy-start.11 = (f32[2,3,64,128]{3,2,1,0:T(8,128)}, f32[2,3,64,128]{3,2,1,0:T(8,128)S(1)}, u32[]{:S(2)}) copy-start(f32[2,3,64,128]{3,2,1,0:T(8,128)S(1)} %get-tuple-element.390) | copy-start | bytes 589828
  286.0 16.7 %copy-start.13 = (f32[2,3,64,128]{3,2,1,0:T(8,128)}, f32[2,3,64,128]{3,2,1,0:T(8,128)S(1)}, u32[]{:S(2)}) copy-start(f32[2,3,64,128]{3,2,1,0:T(8,128)S(1)} %get-tuple-element.394) | copy-start | bytes 589828
  287.5 15.5 %copy-start.15 = (f32[2,3,64,128]{3,2,1,0:T(8,128)}, f32[2,3,64,128]{3,2,1,0:T(8,128)S(1)}, u32[]{:S(2)}) copy-start(f32[2,3,64,128]{3,2,1,0:T(8,128)S(1)} %get-tuple-element.398) | copy-start | bytes 589828
  316.5 15.8 %copy-start.30 = (bf16[1,256,384]{1,2,0:T(8,128)(2,1)}, bf16[1,256,384]{1,2,0:T(8,128)(2,1)S(1)}, u32[]{:S(2)}) copy-start(bf16[1,256,384]{1,2,0:T(8,128)(2,1)S(1)} %copy.1014) | copy-start | bytes 589828
  433.0 65.6 %all-to-all-start.3 = ((bf16[8,128,384]{1,2,0:T(8,128)(2,1)}), bf16[8,128,384]{1,2,0:T(8,128)(2,1)}, u32[]{:S(2)}, u32[]{:S(2)}) async-start(bf16[8,128,384]{1,2,0:T(8,128)(2,1)} %copy.1214), calls=%async_computation.3 | async-start | bytes 1572864 | tf_op jit(solution)/shard_map/all_to_all | solution.py:136
  439.2 320.7 %all-reduce.7.cloned.1.call-start = ((), (), s32[]{:S(2)}) async-start(), calls=%async_computation.6 | async-start | bytes 3145728
  445.7 42.6 %collective-permute-start.3 = (bf16[2,64,384]{1,2,0:T(8,128)(2,1)}, bf16[2,64,384]{1,2,0:T(8,128)(2,1)}, u32[]{:S(2)}, u32[]{:S(2)}) collective-permute-start(bf16[2,64,384]{1,2,0:T(8,128)(2,1)} %get-tuple-element.348), channel_id=1, source_target_pairs={{8,0},{16,8},{24,16},{32,24},{40,32},{48,40},{56,48},{64,56},{72,6... | collective-permute-start | bytes 294920 | tf_op jit(solution)/shard_map/ppermute | solution.py:21
  447.0 41.3 %collective-permute-start.2 = (bf16[2,64,384]{1,2,0:T(8,128)(2,1)}, bf16[2,64,384]{1,2,0:T(8,128)(2,1)}, u32[]{:S(2)}, u32[]{:S(2)}) collective-permute-start(bf16[2,64,384]{1,2,0:T(8,128)(2,1)} %get-tuple-element.347), channel_id=1, source_target_pairs={{0,8},{8,16},{16,24},{24,32},{32,40},{40,48},{48,56},{56,64},{64,7... | collective-permute-start | bytes 294920 | tf_op jit(solution)/shard_map/ppermute | solution.py:18
  498.6 15.9 %all-to-all-start.4 = ((bf16[8,128,384]{1,2,0:T(8,128)(2,1)}), bf16[8,128,384]{1,2,0:T(8,128)(2,1)S(1)}, u32[]{:S(2)}, u32[]{:S(2)}) async-start(bf16[8,128,384]{1,2,0:T(8,128)(2,1)} %copy_bitcast_fusion.1), calls=%async_computation.4 | async-start | bytes 1572864 | tf_op jit(solution)/shard_map/all_to_all | solution.py:137
  514.5 16.6 %all-to-all-start.5 = ((bf16[8,128,384]{1,2,0:T(8,128)(2,1)}), bf16[8,128,384]{1,2,0:T(8,128)(2,1)S(1)}, u32[]{:S(2)}, u32[]{:S(2)}) async-start(bf16[8,128,384]{1,2,0:T(8,128)(2,1)} %copy_bitcast_fusion), calls=%async_computation.5 | async-start | bytes 1572864 | tf_op jit(solution)/shard_map/all_to_all | solution.py:138
  (202 other events, 689.6 us)
Sparse Core Ops, SparseCore 0:
  488.4 271.3 all-reduce.6
where the time goes:
time: 782 us; the launch traced here: 770 us
  waiting for transfers between devices  250 us (32%)
  blocking collectives  190 us (24%)
  local copies, waits for them, and re-layouts  157 us (20%)
  matrix products  63.4 us (8%)
  starting transfers between devices  48.8 us (6%)
  other arithmetic  43.1 us (6%)
  between operations  18.1 us (2%)
    unnamed x2, waiting for transfers between devices  228 us
    all_gather x1, blocking collectives, body(): lax.all_gather(text_k, 'frame', axis=1, tiled=True)  96.9 us
    all_gather x1, blocking collectives, body(): lax.all_gather(text_v, 'frame', axis=1, tiled=True)  92.7 us
    unnamed x450, local copies, waits for them, and re-layouts  36 us
    dot_general x16, matrix products, attend_back(): jnp.einsum('hqk,khd->qhd', dscore, keys, preferred_element_type=jnp.float32)  19.7 us
  transfers between devices with their start and end apart: 11, of which 4 were waited for; matrix products, arithmetic and copies ran while one was open for 17% of the time, Pallas kernels for 0%

commit v1 on v0

v1 whole, which is shorter than its diff:
```python
import math

import jax
import jax.numpy as jnp
from jax import lax
from jax.experimental import pallas as pl
from jax.experimental.pallas import tpu as pltpu
from jax.sharding import PartitionSpec as P

HD = 128
FT = 64
NSEG = 4
TXT = 128
NU = 8
NX = 4
NZ = 16
NF = NX * NZ
HEADS = 3
W = HEADS * HD
TOK = 128
ROWS = NU * TOK
EXT = ROWS + 2 * FT
SCALE = HD ** -0.5
EXP2 = SCALE * math.log2(math.e)
MESH = pl.DeviceIdType.MESH
VMEM_LIMIT = 56 * 1024 * 1024


def place():
    f = lax.axis_index("frame")
    u = lax.axis_index("uly")
    return f, u, lax.div(f, NZ), lax.rem(f, NZ)


def uly_peer(f, u, d):
    return (f, lax.rem(u + d, NU))


def z_peer(x, z, u, d):
    return (x * NZ + lax.rem(z + d, NZ), u)


def x_peer(f, u, d):
    return (lax.rem(f + NZ * d, NF), u)


def meet(f, u, x, z):
    barrier = pltpu.get_barrier_semaphore()
    peers = [uly_peer(f, u, d) for d in range(1, NU)]
    peers += [z_peer(x, z, u, d) for d in range(1, NZ)]
    peers += [x_peer(f, u, d) for d in range(1, NX)]
    peers += [(lax.rem(f + 1, NF), u), (lax.rem(f + NF - 1, NF), u)]
    for peer in peers:
        pl.semaphore_signal(barrier, inc=1, device_id=peer, device_id_type=MESH)
    pl.semaphore_wait(barrier, len(peers))


def remote(src, dst, send, recv, peer):
    return pltpu.make_async_remote_copy(
        src_ref=src, dst_ref=dst, send_sem=send, recv_sem=recv, device_id=peer, device_id_type=MESH
    )


def scatter_heads(q, k, v, text, hq, hk, hv, tg, a_send, a_recv, l_sem, h_send, h_recv, z_send, z_recv, x_send, x_recv):
    f, u, x, z = place()
    meet(f, u, x, z)
    local = [pltpu.make_async_copy(text, tg.at[f], l_sem.at[3])]
    zs = []
    for d in range(1, NZ):
        zs.append(remote(text, tg.at[f], z_send.at[d], z_recv.at[d], z_peer(x, z, u, d)))
    moves = []
    mine = pl.ds(pl.multiple_of(u * W, HD), W)
    for i, (src, dst, off) in enumerate(((k, hk, FT), (v, hv, FT), (q, hq, 0))):
        rows = pl.ds(pl.multiple_of(off + u * TOK, FT), TOK)
        local.append(pltpu.make_async_copy(src.at[:, mine], dst.at[rows], l_sem.at[i]))
        group = []
        for d in (4, 3, 5, 2, 6, 1, 7):
            peer = uly_peer(f, u, d)
            cols = pl.ds(pl.multiple_of(peer[1] * W, HD), W)
            group.append(remote(src.at[:, cols], dst.at[rows], a_send.at[i, d], a_recv.at[i, d], peer))
        moves.append(group)
    for c in zs + local + moves[0] + moves[1] + moves[2]:
        c.start()
    for c in zs:
        c.wait_recv()
    local[0].wait()
    xs = []
    block = pl.ds(x * NZ, NZ)
    for d in range(1, NX):
        xs.append(remote(tg.at[block], tg.at[block], x_send.at[d], x_recv.at[d], x_peer(f, u, d)))
    for c in xs:
        c.start()
    for c in moves[0] + moves[1]:
        c.wait_recv()
    local[1].wait()
    local[2].wait()
    after = (lax.rem(f + 1, NF), u)
    before = (lax.rem(f + NF - 1, NF), u)
    halo = []
    for i, ref in enumerate((hk, hv)):
        halo.append(remote(ref.at[pl.ds(FT, FT)], ref.at[pl.ds(FT + ROWS, FT)], h_send.at[i, 0], h_recv.at[i, 0], before))
        halo.append(remote(ref.at[pl.ds(ROWS, FT)], ref.at[pl.ds(0, FT)], h_send.at[i, 1], h_recv.at[i, 1], after))
    for c in halo:
        c.start()
    for c in moves[2]:
        c.wait_recv()
    local[3].wait()
    for c in halo + xs:
        c.wait_recv()
    for c in zs + moves[0] + moves[1] + moves[2] + xs + halo:
        c.wait_send()


def dot(a, b, ca, cb):
    return lax.dot_general(a, b, (((ca,), (cb,)), ((), ())), preferred_element_type=jnp.float32)


def softmax(scores):
    top = jnp.max(scores, axis=-1, keepdims=True)
    e = jnp.exp2((scores - top) * EXP2)
    return e * (1.0 / jnp.sum(e, axis=-1, keepdims=True))


def attention(lens, segs, hq, hk, hv, tg, dq, dk, dv, edge, halo, gout, t32, kv32, kv16, acc_k, acc_v, acc_t):
    f = lax.axis_index("frame")
    b0 = segs[0]
    b1 = b0 + segs[1]
    b2 = b1 + segs[2]
    b3 = b2 + segs[3]
    for h in range(HEADS):
        t32[h] = tg[:, :, h * HD : (h + 1) * HD].reshape(NF * 16, HD).astype(jnp.float32)
        for c in range(2):
            for s in range(NSEG):
                for t in range(2):
                    kv32[h, c, s, pl.ds(t, NF, stride=2), :] = t32[h, pl.ds(c * 8 + s * 2 + t, NF, stride=16), :]
    kv16[...] = kv32[...].astype(jnp.bfloat16)
    acc_k[...] = jnp.zeros_like(acc_k)
    acc_v[...] = jnp.zeros_like(acc_v)
    acc_t[...] = jnp.zeros_like(acc_t)
    row = lax.broadcasted_iota(jnp.int32, (2 * FT, 4 * FT), 0)
    col = lax.broadcasted_iota(jnp.int32, (2 * FT, 4 * FT), 1)
    tcol = lax.broadcasted_iota(jnp.int32, (FT, TXT), 1)

    def step(p, carry):
        low = jnp.logical_and(f == 0, p == 0).astype(jnp.int32)
        high = jnp.logical_and(f == NF - 1, p == ROWS // TOK - 1).astype(jnp.int32)
        bad = ((col < FT) & (row >= FT * (1 - low))) | ((col >= 3 * FT) & (row < FT * (1 + high)))
        qr = pl.ds(pl.multiple_of(p * TOK, TOK), TOK)
        kr = pl.ds(pl.multiple_of(p * TOK, TOK), 4 * FT)
        seg = []
        for a in range(2):
            frame = f * (ROWS // FT) + 2 * p + a
            s = sum((frame >= b).astype(jnp.int32) for b in (b0, b1, b2, b3))
            seg.append((s, lens[s]))
        for h in range(HEADS):
            cs = slice(h * HD, (h + 1) * HD)
            q = hq[qr, cs]
            k = hk[kr, cs]
            v = hv[kr, cs]
            probs = softmax(jnp.where(bad, -1e30, dot(q, k, 1, 1)))
            rounded = probs.astype(jnp.bfloat16)
            self_out = dot(rounded, v, 1, 0)
            parts = []
            for a in range(2):
                s, n = seg[a]
                tk = kv16[h, 0, s]
                tv = kv16[h, 1, s]
                qa = q[a * FT : (a + 1) * FT]
                cp = softmax(jnp.where(tcol < n, dot(qa, tk, 1, 1), -1e30))
                cr = cp.astype(jnp.bfloat16)
                parts.append((s, tk, tv, qa, cp, cr, dot(cr, tv, 1, 0)))
            cross_out = jnp.concatenate([parts[0][-1], parts[1][-1]], axis=0)
            g = (self_out + cross_out).astype(jnp.bfloat16)
            g32 = g.astype(jnp.float32)
            s_delta = jnp.sum(g32 * self_out, axis=-1, keepdims=True)
            c_delta = jnp.sum(g32 * cross_out, axis=-1, keepdims=True)
            ds = (probs * (dot(g, v, 1, 1) - s_delta)).astype(jnp.bfloat16)
            dq_self = dot(ds, k, 1, 0)
            acc_k[h, kr] += dot(ds, q, 0, 0)
            acc_v[h, kr] += dot(rounded, g, 0, 0)
            dq_cross = []
            for a in range(2):
                s, tk, tv, qa, cp, cr, _ = parts[a]
                half = slice(a * FT, (a + 1) * FT)
                ga = g[half]
                dsc = (cp * (dot(ga, tv, 1, 1) - c_delta[half])).astype(jnp.bfloat16)
                dq_cross.append(dot(dsc, tk, 1, 0))
                acc_t[h, 0, s] += dot(dsc, qa, 0, 0)
                acc_t[h, 1, s] += dot(cr, ga, 0, 0)
            total = dq_self + jnp.concatenate(dq_cross, axis=0)
            dq[qr, cs] = (total * SCALE).astype(jnp.bfloat16)
        return carry

    lax.fori_loop(0, ROWS // TOK, step, 0)
    for h in range(HEADS):
        cs = slice(h * HD, (h + 1) * HD)
        for i, (acc, out, scale) in enumerate(((acc_k, dk, SCALE), (acc_v, dv, 1.0))):
            out[:, cs] = (acc[h, FT : FT + ROWS] * scale).astype(jnp.bfloat16)
            edge[2 * i, :, cs] = acc[h, FT : 2 * FT] * scale
            edge[2 * i + 1, :, cs] = acc[h, ROWS : ROWS + FT] * scale
            halo[2 * i, :, cs] = (acc[h, 0:FT] * scale).astype(jnp.bfloat16)
            halo[2 * i + 1, :, cs] = (acc[h, FT + ROWS : EXT] * scale).astype(jnp.bfloat16)
        for c in range(2):
            scale = SCALE if c == 0 else 1.0
            for s in range(NSEG):
                for t in range(2):
                    t32[h, pl.ds(c * 8 + s * 2 + t, NF, stride=16), :] = acc_t[h, c, s, pl.ds(t, NF, stride=2), :] * scale
        gout[:, :, cs] = t32[h].astype(jnp.bfloat16).reshape(NF, 16, HD)


def gather_heads(
    dq, dk, dv, edge, halo, gt, oq, ok, ov, og,
    kbuf, vbuf, hrecv, rx, s1, rz,
    a_send, a_recv, l_sem, h_send, h_recv, z_send, z_recv, x_send, x_recv,
):
    f, u, x, z = place()
    meet(f, u, x, z)
    after = (lax.rem(f + 1, NF), u)
    before = (lax.rem(f + NF - 1, NF), u)
    hs = []
    for i in range(2):
        hs.append(remote(halo.at[2 * i], hrecv.at[2 * i + 1], h_send.at[2 * i], h_recv.at[2 * i], before))
        hs.append(remote(halo.at[2 * i + 1], hrecv.at[2 * i], h_send.at[2 * i + 1], h_recv.at[2 * i + 1], after))
    xs = []
    for d in range(1, NX):
        peer = x_peer(f, u, d)
        block = pl.ds(lax.rem(x + d, NX) * NZ, NZ)
        xs.append(remote(gt.at[block], rx.at[d - 1], x_send.at[d], x_recv.at[d], peer))
    stage = [
        pltpu.make_async_copy(dk, kbuf, l_sem.at[0]),
        pltpu.make_async_copy(dv, vbuf, l_sem.at[1]),
    ]
    moves, local = [], []
    mine = pl.ds(pl.multiple_of(u * W, HD), W)
    own = pl.ds(pl.multiple_of(u * TOK, TOK), TOK)
    for i, (src, dst) in enumerate(((dq, oq), (kbuf, ok), (vbuf, ov))):
        local.append(pltpu.make_async_copy(src.at[own], dst.at[:, mine], l_sem.at[2 + i]))
        group = []
        for d in (4, 3, 5, 2, 6, 1, 7):
            peer = uly_peer(f, u, d)
            rows = pl.ds(pl.multiple_of(peer[1] * TOK, TOK), TOK)
            group.append(remote(src.at[rows], dst.at[:, mine], a_send.at[i, d], a_recv.at[i, d], peer))
        moves.append(group)
    for c in hs + xs + stage + moves[0] + local[:1]:
        c.start()
    for c in hs:
        c.wait_recv()
    for c in stage:
        c.wait()
    kbuf[0:FT] = (edge[0] + hrecv[0].astype(jnp.float32)).astype(jnp.bfloat16)
    kbuf[ROWS - FT : ROWS] = (edge[1] + hrecv[1].astype(jnp.float32)).astype(jnp.bfloat16)
    vbuf[0:FT] = (edge[2] + hrecv[2].astype(jnp.float32)).astype(jnp.bfloat16)
    vbuf[ROWS - FT : ROWS] = (edge[3] + hrecv[3].astype(jnp.float32)).astype(jnp.bfloat16)
    for c in moves[1] + moves[2] + local[1:]:
        c.start()
    for c in xs:
        c.wait_recv()
    total = gt[pl.ds(x * NZ, NZ)].astype(jnp.float32)
    for d in range(1, NX):
        total = total + rx[d - 1].astype(jnp.float32)
    s1[...] = total.astype(jnp.bfloat16)
    zs = []
    for d in range(1, NZ):
        zs.append(remote(s1.at[lax.rem(z + d, NZ)], rz.at[d - 1], z_send.at[d], z_recv.at[d], z_peer(x, z, u, d)))
    for c in zs:
        c.start()
    for c in zs:
        c.wait_recv()
    last = s1[z].astype(jnp.float32)
    for d in range(1, NZ):
        last = last + rz[d - 1].astype(jnp.float32)
    og[...] = last
    for g in moves:
        for c in g:
            c.wait_recv()
    for c in local:
        c.wait()
    for c in hs + xs + zs + moves[0] + moves[1] + moves[2]:
        c.wait_send()


def body(queries, keys, values, text_k, text_v, text_len, seg_frames):
    bf16, f32 = jnp.bfloat16, jnp.float32
    hbm = pl.BlockSpec(memory_space=pl.ANY)
    vmem = pl.BlockSpec(memory_space=pltpu.VMEM)
    smem = pl.BlockSpec(memory_space=pltpu.SMEM)
    dma = pltpu.SemaphoreType.DMA
    S = jax.ShapeDtypeStruct
    text = jnp.concatenate([text_k.reshape(8, W), text_v.reshape(8, W)], axis=0)
    hq, hk, hv, tg = pl.pallas_call(
        scatter_heads,
        out_shape=(S((ROWS, W), bf16), S((EXT, W), bf16), S((EXT, W), bf16), S((NF, 16, W), bf16)),
        in_specs=[hbm, hbm, hbm, hbm],
        out_specs=(hbm, hbm, hbm, hbm),
        scratch_shapes=[
            dma((3, NU)), dma((3, NU)), dma((4,)), dma((2, 2)), dma((2, 2)),
            dma((NZ,)), dma((NZ,)), dma((NX,)), dma((NX,)),
        ],
        compiler_params=pltpu.CompilerParams(collective_id=0, has_side_effects=True, vmem_limit_bytes=VMEM_LIMIT),
        name="scatter_heads",
    )(queries, keys, values, text)
    dq, dk, dv, edge, halo, gt = pl.pallas_call(
        attention,
        out_shape=(
            S((ROWS, W), bf16), S((ROWS, W), bf16), S((ROWS, W), bf16),
            S((4, FT, W), f32), S((4, FT, W), bf16), S((NF, 16, W), bf16),
        ),
        in_specs=[smem, smem, vmem, vmem, vmem, vmem],
        out_specs=(vmem,) * 6,
        scratch_shapes=[
            pltpu.VMEM((HEADS, NF * 16, HD), f32),
            pltpu.VMEM((HEADS, 2, NSEG, TXT, HD), f32),
            pltpu.VMEM((HEADS, 2, NSEG, TXT, HD), bf16),
            pltpu.VMEM((HEADS, EXT, HD), f32),
            pltpu.VMEM((HEADS, EXT, HD), f32),
            pltpu.VMEM((HEADS, 2, NSEG, TXT, HD), f32),
        ],
        compiler_params=pltpu.CompilerParams(vmem_limit_bytes=VMEM_LIMIT),
        name="attention",
    )(text_len, seg_frames, hq, hk, hv, tg)
    oq, ok, ov, og = pl.pallas_call(
        gather_heads,
        out_shape=(S((TOK, NU * W), bf16),) * 3 + (S((16, W), f32),),
        in_specs=[hbm, hbm, hbm, vmem, vmem, vmem],
        out_specs=(hbm, hbm, hbm, vmem),
        scratch_shapes=[
            pltpu.VMEM((ROWS, W), bf16), pltpu.VMEM((ROWS, W), bf16), pltpu.VMEM((4, FT, W), bf16),
            pltpu.VMEM((NX - 1, NZ, 16, W), bf16), pltpu.VMEM((NZ, 16, W), bf16), pltpu.VMEM((NZ - 1, 16, W), bf16),
            dma((3, NU)), dma((3, NU)), dma((5,)), dma((4,)), dma((4,)),
            dma((NZ,)), dma((NZ,)), dma((NX,)), dma((NX,)),
        ],
        compiler_params=pltpu.CompilerParams(collective_id=1, has_side_effects=True, vmem_limit_bytes=VMEM_LIMIT),
        name="gather_heads",
    )(dq, dk, dv, edge, halo, gt)
    og = og.reshape(2, NSEG, 2, W)
    return oq, ok, ov, og[0], og[1]


def solution(mesh):
    rows = P(("frame", "uly"), None)
    text = P(None, "frame", "uly")
    return jax.shard_map(
        body,
        mesh=mesh,
        in_specs=(rows, rows, rows, text, text, P(), P()),
        out_specs=(rows, rows, rows, text, text),
        check_vma=False,
    )
```

time: 782 us -> 119 us (0.15)
  the two profiles are of different devices: /device:TPU:24 before, /device:TPU:1 now
where the time goes in v1:
time: 119 us; the launch traced here: 118 us
  Pallas kernels  110 us (92%)
  local copies, waits for them, and re-layouts  7.11 us (6%)
    pallas_call x1, Pallas kernels, body(): pl.pallas_call(scatter_heads, out_shape=(S((ROWS, W), bf16), S((EXT, W),...  44.9 us
    pallas_call x1, Pallas kernels, body(): pl.pallas_call(gather_heads, out_shape=(S((TOK, NU * W), bf16),) * 3 + (S...  34.6 us
    pallas_call x1, Pallas kernels, body(): pl.pallas_call(attention, out_shape=(S((ROWS, W), bf16), S((ROWS, W), bf1...  30.5 us
    unnamed x9, local copies, waits for them, and re-layouts  4.44 us

profile of v1, /device:TPU:1, one launch (start us, length us, event | category | flops | bytes accessed | tf_op | source)
XLA Modules:
  0.0 118.4 jit_solution(16926133464168887851)
XLA Ops:
  0.6 0.0 copy-start.2
  0.6 0.7 reshape.21
  1.3 0.0 copy-done.2
  1.4 0.6 pad_maximum_fusion.text
  2.0 44.9 %scatter_heads.1 = (bf16[1024,384]{1,0:T(8,128)(2,1)}, bf16[1152,384]{1,0:T(8,128)(2,1)}, bf16[1152,384]{1,0:T(8,128)(2,1)}, bf16[64,16,384]{2,1,0:T(8,128)(2,1)}) custom-call(bf16[128,3072]{1,0:T(8,128)(2,1)} %q.1, bf16[128,3072]{1,0:T(8,128)(2,1)} %k.1, bf16[128,3072]{1,0:T(8,128)(2,1)} %v.1, bf16[16,384]{1,0:T(8,128)(2,1)} %pad_maximum_fusion.text), custom_call_target="tpu_custom_call" | custom-call | tf_op jit(solution)/shard_map/scatter_heads/pallas_call | solution.py:290
  46.8 30.5 %attention.1 = (bf16[1024,384]{1,0:T(8,128)(2,1)}, bf16[1024,384]{1,0:T(8,128)(2,1)}, bf16[1024,384]{1,0:T(8,128)(2,1)}, f32[4,64,384]{2,1,0:T(8,128)}, bf16[4,6...) custom-call(s32[4]{0:T(128)} %lens.1, s32[4]{0:T(128)} %segs.1, bf16[1024,384]{1,0:T(8,128)(2,1)} %get-tuple-element.19.hq, ...), custom_call_target="tpu_custom_call" | custom-call | tf_op jit(solution)/shard_map/attention/pallas_call | solution.py:302
  77.3 34.6 %gather_heads.1 = (bf16[128,3072]{1,0:T(8,128)(2,1)}, bf16[128,3072]{1,0:T(8,128)(2,1)}, bf16[128,3072]{1,0:T(8,128)(2,1)}, f32[16,384]{1,0:T(8,128)}) custom-call(bf16[1024,384]{1,0:T(8,128)(2,1)} %get-tuple-element.23.dq, bf16[1024,384]{1,0:T(8,128)(2,1)} %get-tuple-element.24.dk, bf16[1024,384]{1,0:T(8,128)(2,1)} %get-tuple-element.25.dv, ...), custom_call_target="tpu_custom_call" | custom-call | tf_op jit(solution)/shard_map/gather_heads/pallas_call | solution.py:321
  112.0 0.7 fusion
  112.7 0.6 squeeze.7
  113.3 0.6 squeeze.6
  113.9 0.0 copy-start.1
  113.9 2.1 %copy.15 = bf16[128,3072]{1,0:T(8,128)(2,1)} copy(bf16[128,3072]{1,0:T(8,128)(2,1)} %get-tuple-element.40) | data formatting | bytes 1572864
  116.1 0.0 copy-done.1
  116.1 0.0 copy-start
  116.1 0.9 copy.16
  116.9 0.5 copy-done
  117.5 0.9 copy.17
  (1 shorter events, 0.0 us)
Async XLA Ops:
  0.6 0.7 copy-start.2
  113.9 2.1 %copy-start.1 = (bf16[128,3072]{1,0:T(8,128)(2,1)S(1)}, bf16[128,3072]{1,0:T(8,128)(2,1)}, u32[]{:S(2)}) copy-start(bf16[128,3072]{1,0:T(8,128)(2,1)} %get-tuple-element.41) | copy-start | bytes 2359300
  116.1 1.4 %copy-start = (bf16[128,3072]{1,0:T(8,128)(2,1)S(1)}, bf16[128,3072]{1,0:T(8,128)(2,1)}, u32[]{:S(2)}) copy-start(bf16[128,3072]{1,0:T(8,128)(2,1)} %get-tuple-element.42) | copy-start | bytes 2359300

commit v2 on v0

v2 whole, which is shorter than its diff:
```python
import math

import jax
import jax.numpy as jnp
from jax import lax
from jax.experimental import pallas as pl
from jax.experimental.pallas import tpu as pltpu
from jax.sharding import PartitionSpec as P

HD = 128
FT = 64
NSEG = 4
TXT = 128
NU = 8
NX = 4
NZ = 16
NF = NX * NZ
HEADS = 3
W = HEADS * HD
TOK = 128
ROWS = NU * TOK
EXT = ROWS + 2 * FT
TILES = EXT // TOK
SCALE = HD ** -0.5
EXP2 = SCALE * math.log2(math.e)
MESH = pl.DeviceIdType.MESH
VMEM_LIMIT = 56 * 1024 * 1024
FAR_FIRST = (4, 3, 5, 2, 6, 1, 7)
BF16 = jnp.bfloat16
F32 = jnp.float32


def place():
    f = lax.axis_index("frame")
    u = lax.axis_index("uly")
    return f, u, lax.div(f, NZ), lax.rem(f, NZ)


def uly_peer(f, u, d):
    return (f, lax.rem(u + d, NU))


def z_peer(x, z, u, d):
    return (x * NZ + lax.rem(z + d, NZ), u)


def x_peer(f, u, d):
    return (lax.rem(f + NZ * d, NF), u)


def meet(f, u, x, z):
    barrier = pltpu.get_barrier_semaphore()
    peers = [uly_peer(f, u, d) for d in range(1, NU)]
    peers += [z_peer(x, z, u, d) for d in range(1, NZ)]
    peers += [x_peer(f, u, d) for d in range(1, NX)]
    peers += [(lax.rem(f + 1, NF), u), (lax.rem(f + NF - 1, NF), u)]
    for peer in peers:
        pl.semaphore_signal(barrier, inc=1, device_id=peer, device_id_type=MESH)
    pl.semaphore_wait(barrier, len(peers))


def remote(src, dst, send, recv, peer):
    return pltpu.make_async_remote_copy(
        src_ref=src, dst_ref=dst, send_sem=send, recv_sem=recv, device_id=peer, device_id_type=MESH
    )


def dot(a, b, ca, cb):
    return lax.dot_general(a, b, (((ca,), (cb,)), ((), ())), preferred_element_type=F32)


def softmax(scores):
    top = jnp.max(scores, axis=0, keepdims=True)
    e = jnp.exp2((scores - top) * EXP2)
    return e * (1.0 / jnp.sum(e, axis=0, keepdims=True))


def bounds_of(segs):
    b0 = segs[0]
    b1 = b0 + segs[1]
    b2 = b1 + segs[2]
    return b0, b1, b2


def segment(frame, bounds):
    return sum((frame >= b).astype(jnp.int32) for b in bounds)


def text_in(tg, t32, kv32, tkv, tkvT):
    for h in range(HEADS):
        t32[...] = tg[h].reshape(NF * 16, HD).astype(F32)
        for c in range(2):
            for s in range(NSEG):
                for t in range(2):
                    kv32[c, s, pl.ds(t, NF, stride=2), :] = t32[pl.ds(c * 8 + s * 2 + t, NF, stride=16), :]
                part = kv32[c, s]
                tkv[h, c, s] = part.astype(BF16)
                tkvT[h, c, s] = part.T.astype(BF16)


def turn(src, dst, tiles):
    for t in tiles:
        dst[:, t * TOK : (t + 1) * TOK] = src[t * TOK : (t + 1) * TOK, :].T


def pairs_step(pairs, f, lens, bounds, hq, hk, hv, kT, vT, tkv, tkvT, dq, acc_k, acc_v, sc, pc, gT):
    row = lax.broadcasted_iota(jnp.int32, (4 * FT, 2 * FT), 0)
    lane = lax.broadcasted_iota(jnp.int32, (4 * FT, 2 * FT), 1)
    trow = lax.broadcasted_iota(jnp.int32, (TXT, 2 * FT), 0)
    left = lax.broadcasted_iota(jnp.int32, (TXT, 2 * FT), 1) < FT
    work = []
    for p in pairs:
        low = jnp.logical_and(f == 0, p == 0).astype(jnp.int32)
        high = jnp.logical_and(f == NF - 1, p == ROWS // TOK - 1).astype(jnp.int32)
        bad = ((row < FT) & (lane >= FT * (1 - low))) | ((row >= 3 * FT) & (lane < FT * (1 + high)))
        qr = pl.ds(pl.multiple_of(p * TOK, TOK), TOK)
        kr = pl.ds(pl.multiple_of(p * TOK, TOK), 4 * FT)
        s0 = segment(f * (ROWS // FT) + 2 * p, bounds)
        s1 = segment(f * (ROWS // FT) + 2 * p + 1, bounds)
        n = jnp.where(left, lens[s0], lens[s1])
        work.append((bad, qr, kr, s0, s1, n))
    qs = [hq[w[1], :] for w in work]
    ks = [hk[w[2], :] for w in work]
    vs = [hv[w[2], :] for w in work]
    ss = [dot(k, q, 1, 1) for k, q in zip(ks, qs)]
    cs = [
        jnp.where(left, dot(tkv[0, w[3]], q, 1, 1), dot(tkv[0, w[4]], q, 1, 1)) for w, q in zip(work, qs)
    ]
    ps = [softmax(jnp.where(w[0], -1e30, s)) for w, s in zip(work, ss)]
    cps = [softmax(jnp.where(trow < w[5], c, -1e30)) for w, c in zip(work, cs)]
    p16 = [p.astype(BF16) for p in ps]
    cp16 = [c.astype(BF16) for c in cps]
    so = [dot(vT[:, w[2]], p, 1, 0) for w, p in zip(work, p16)]
    co = [
        jnp.where(left, dot(tkvT[1, w[3]], c, 1, 0), dot(tkvT[1, w[4]], c, 1, 0)) for w, c in zip(work, cp16)
    ]
    g16 = [(a + b).astype(BF16) for a, b in zip(so, co)]
    sd = [jnp.sum(g.astype(F32) * a, axis=0, keepdims=True) for g, a in zip(g16, so)]
    cd = [jnp.sum(g.astype(F32) * a, axis=0, keepdims=True) for g, a in zip(g16, co)]
    ds = [(p * (dot(v, g, 1, 0) - d)).astype(BF16) for p, v, g, d in zip(ps, vs, g16, sd)]
    dcs = [
        (c * (jnp.where(left, dot(tkv[1, w[3]], g, 1, 0), dot(tkv[1, w[4]], g, 1, 0)) - d)).astype(BF16)
        for c, w, g, d in zip(cps, work, g16, cd)
    ]
    dqs = [
        dot(kT[:, w[2]], s, 1, 0) + jnp.where(left, dot(tkvT[0, w[3]], c, 1, 0), dot(tkvT[0, w[4]], c, 1, 0))
        for w, s, c in zip(work, ds, dcs)
    ]
    dks = [acc_k[w[2], :] + dot(s, q, 1, 0) for w, s, q in zip(work, ds, qs)]
    dvs = [acc_v[w[2], :] + dot(p, g, 1, 1) for w, p, g in zip(work, p16, g16)]
    for i, w in enumerate(work):
        dq[w[1], :] = (dqs[i] * SCALE).T.astype(BF16)
        acc_k[w[2], :] = dks[i]
        acc_v[w[2], :] = dvs[i]
        sc[:, w[1]] = dcs[i]
        pc[:, w[1]] = cp16[i]
        gT[:, w[1]] = g16[i]


def text_out(f, bounds, hq, sc, pc, gT, t32, kv32, gt):
    frame = f * (ROWS // FT) + lax.broadcasted_iota(jnp.int32, (16, ROWS), 1) // FT
    seg = segment(frame, bounds)
    q = hq[...]
    g = gT[...]
    for s in range(NSEG):
        on = jnp.broadcast_to((seg == s).astype(F32).astype(BF16)[0:1], (TXT, ROWS))
        kv32[0, s] = dot(sc[...] * on, q, 1, 0) * SCALE
        kv32[1, s] = dot(pc[...] * on, g, 1, 1)
    for c in range(2):
        for s in range(NSEG):
            for t in range(2):
                t32[pl.ds(c * 8 + s * 2 + t, NF, stride=16), :] = kv32[c, s, pl.ds(t, NF, stride=2), :]
    gt[...] = t32[...].astype(BF16).reshape(NF, 16, HD)


def fused(
    lens, segs, q, k, v, tk_in, tv_in, oq, ok, ov, ogk, ogv,
    slab32, slab, hq, hk, hv, tg, t32, kv32, tkv, tkvT, kT, vT, acc_k, acc_v, sc, pc, gT,
    dq, dk, dv, hsend, hrecv, gt, rx, s1, rz,
    a_send, a_recv, l_sem, h_send, h_recv, z_send, z_recv, x_send, x_recv,
    b_send, b_recv, m_sem, e_send, e_recv, w_send, w_recv, y_send, y_recv,
):
    f, u, x, z = place()
    bounds = bounds_of(segs)
    after = (lax.rem(f + 1, NF), u)
    before = (lax.rem(f + NF - 1, NF), u)
    for s in range(NSEG):
        slab32[2 * s : 2 * s + 2, :] = tk_in[s].astype(F32)
        slab32[8 + 2 * s : 8 + 2 * s + 2, :] = tv_in[s].astype(F32)
    for h in range(HEADS):
        slab[h] = slab32[:, h * HD : (h + 1) * HD].astype(BF16)
    meet(f, u, x, z)

    own_text = pltpu.make_async_copy(slab, tg.at[:, f], l_sem.at[0, 3])
    zs = [remote(slab, tg.at[:, f], z_send.at[d], z_recv.at[d], z_peer(x, z, u, d)) for d in range(1, NZ)]
    block = pl.ds(x * NZ, NZ)
    xs = [
        remote(tg.at[:, block], tg.at[:, block], x_send.at[d], x_recv.at[d], x_peer(f, u, d)) for d in range(1, NX)
    ]

    def arrivals(h):
        local, moves = [], []
        for i, (src, dst, off) in enumerate(((k, hk, FT), (v, hv, FT), (q, hq, 0))):
            rows = pl.ds(pl.multiple_of(off + u * TOK, FT), TOK)
            mine = pl.ds(pl.multiple_of(u * W + h * HD, HD), HD)
            local.append(pltpu.make_async_copy(src.at[:, mine], dst.at[h, rows], l_sem.at[h, i]))
            for d in FAR_FIRST:
                peer = uly_peer(f, u, d)
                cols = pl.ds(pl.multiple_of(peer[1] * W + h * HD, HD), HD)
                moves.append(remote(src.at[:, cols], dst.at[h, rows], a_send.at[h, i, d], a_recv.at[h, i, d], peer))
        return local, moves

    def halo_in(h):
        out = []
        for i, ref in enumerate((hk, hv)):
            lo, hi = ref.at[h, pl.ds(FT, FT)], ref.at[h, pl.ds(ROWS, FT)]
            out.append(remote(lo, ref.at[h, pl.ds(FT + ROWS, FT)], h_send.at[h, i, 0], h_recv.at[h, i, 0], before))
            out.append(remote(hi, ref.at[h, pl.ds(0, FT)], h_send.at[h, i, 1], h_recv.at[h, i, 1], after))
        return out

    def halo_out(h):
        out = []
        for i in range(2):
            out.append(remote(hsend.at[h, 2 * i], hrecv.at[h, 2 * i + 1], e_send.at[h, 2 * i], e_recv.at[h, 2 * i], before))
            out.append(
                remote(hsend.at[h, 2 * i + 1], hrecv.at[h, 2 * i], e_send.at[h, 2 * i + 1], e_recv.at[h, 2 * i + 1], after)
            )
        return out

    def returns(h, i):
        src, dst = ((dq, oq), (dk, ok), (dv, ov))[i]
        cols = pl.ds(pl.multiple_of(u * W + h * HD, HD), HD)
        own = pl.ds(pl.multiple_of(u * TOK, TOK), TOK)
        local = pltpu.make_async_copy(src.at[h, own], dst.at[:, cols], m_sem.at[h, i])
        moves = []
        for d in FAR_FIRST:
            peer = uly_peer(f, u, d)
            rows = pl.ds(pl.multiple_of(peer[1] * TOK, TOK), TOK)
            moves.append(remote(src.at[h, rows], dst.at[:, cols], b_send.at[h, i, d], b_recv.at[h, i, d], peer))
        return local, moves

    def text_x(h):
        out = []
        for d in range(1, NX):
            part = pl.ds(lax.rem(x + d, NX) * NZ, NZ)
            out.append(remote(gt.at[h, part], rx.at[h, d - 1], y_send.at[h, d], y_recv.at[h, d], x_peer(f, u, d)))
        return out

    def text_z(h):
        return [
            remote(s1.at[h, lax.rem(z + d, NZ)], rz.at[h, d - 1], w_send.at[h, d], w_recv.at[h, d], z_peer(x, z, u, d))
            for d in range(1, NZ)
        ]

    def finish_edges(h):
        for c in halo_out(h):
            c.wait_recv()
        for i, (acc, out) in enumerate(((acc_k, dk), (acc_v, dv))):
            scale = SCALE if i == 0 else 1.0
            out[h, 0:FT] = (acc[h, FT : 2 * FT] * scale + hrecv[h, 2 * i].astype(F32)).astype(BF16)
            out[h, ROWS - FT : ROWS] = (acc[h, ROWS : ROWS + FT] * scale + hrecv[h, 2 * i + 1].astype(F32)).astype(BF16)
        for i in (1, 2):
            local, moves = returns(h, i)
            local.start()
            for c in moves:
                c.start()

    def text_mid(h):
        for c in text_x(h):
            c.wait_recv()
        total = gt[h, block].astype(F32)
        for d in range(1, NX):
            total = total + rx[h, d - 1].astype(F32)
        s1[h] = total.astype(BF16)
        for c in text_z(h):
            c.start()

    for c in zs:
        c.start()
    own_text.start()
    for h in range(HEADS):
        local, moves = arrivals(h)
        for c in local + moves:
            c.start()
    acc_k[...] = jnp.zeros_like(acc_k)
    acc_v[...] = jnp.zeros_like(acc_v)
    own_text.wait()
    for c in zs:
        c.wait_recv()
    for c in xs:
        c.start()

    for h in range(HEADS):
        local, moves = arrivals(h)
        for c in local:
            c.wait()
        for c in moves:
            c.wait_recv()
        halo = halo_in(h)
        for c in halo:
            c.start()
        turn(hk.at[h], kT, range(1, TILES - 1))
        turn(hv.at[h], vT, range(1, TILES - 1))
        if h == 0:
            for c in xs:
                c.wait_recv()
            text_in(tg, t32, kv32, tkv, tkvT)
        refs = (
            f, lens, bounds, hq.at[h], hk.at[h], hv.at[h], kT, vT, tkv.at[h], tkvT.at[h], dq.at[h],
            acc_k.at[h], acc_v.at[h], sc, pc, gT,
        )

        def inner(i, carry):
            pairs_step((i + 1, i + 4), *refs)
            return carry

        lax.fori_loop(0, 3, inner, 0)
        for c in halo:
            c.wait_recv()
        turn(hk.at[h], kT, (0, TILES - 1))
        turn(hv.at[h], vT, (0, TILES - 1))
        pairs_step((0, 7), *refs)
        for i, acc in enumerate((acc_k, acc_v)):
            scale = SCALE if i == 0 else 1.0
            hsend[h, 2 * i] = (acc[h, 0:FT] * scale).astype(BF16)
            hsend[h, 2 * i + 1] = (acc[h, FT + ROWS : EXT] * scale).astype(BF16)
        for c in halo_out(h):
            c.start()
        local, moves = returns(h, 0)
        local.start()
        for c in moves:
            c.start()
        text_out(f, bounds, hq.at[h], sc, pc, gT, t32, kv32, gt.at[h])
        for c in text_x(h):
            c.start()
        dk[h, FT : ROWS - FT] = (acc_k[h, 2 * FT : ROWS] * SCALE).astype(BF16)
        dv[h, FT : ROWS - FT] = acc_v[h, 2 * FT : ROWS].astype(BF16)
        finish_edges(h)
        if h > 0:
            text_mid(h - 1)
    text_mid(HEADS - 1)
    for h in range(HEADS):
        for c in text_z(h):
            c.wait_recv()
        last = s1[h, z].astype(F32)
        for d in range(1, NZ):
            last = last + rz[h, d - 1].astype(F32)
        cols = slice(h * HD, (h + 1) * HD)
        for s in range(NSEG):
            ogk[s, :, cols] = last[2 * s : 2 * s + 2]
            ogv[s, :, cols] = last[8 + 2 * s : 8 + 2 * s + 2]
    for c in zs + xs:
        c.wait_send()
    for h in range(HEADS):
        for c in arrivals(h)[1] + halo_in(h) + halo_out(h) + text_x(h) + text_z(h):
            c.wait_send()
        for i in range(3):
            local, moves = returns(h, i)
            local.wait()
            for c in moves:
                c.wait()


def body(queries, keys, values, text_k, text_v, text_len, seg_frames):
    hbm = pl.BlockSpec(memory_space=pl.ANY)
    vmem = pl.BlockSpec(memory_space=pltpu.VMEM)
    smem = pl.BlockSpec(memory_space=pltpu.SMEM)
    dma = pltpu.SemaphoreType.DMA
    S = jax.ShapeDtypeStruct
    V = pltpu.VMEM
    H = HEADS
    return pl.pallas_call(
        fused,
        out_shape=(S((TOK, NU * W), BF16),) * 3 + (S((NSEG, 2, W), F32),) * 2,
        in_specs=[smem, smem, hbm, hbm, hbm, vmem, vmem],
        out_specs=(hbm, hbm, hbm, vmem, vmem),
        scratch_shapes=[
            V((16, W), F32), V((H, 16, HD), BF16),
            V((H, ROWS, HD), BF16), V((H, EXT, HD), BF16), V((H, EXT, HD), BF16),
            V((H, NF, 16, HD), BF16), V((NF * 16, HD), F32), V((2, NSEG, TXT, HD), F32),
            V((H, 2, NSEG, TXT, HD), BF16), V((H, 2, NSEG, HD, TXT), BF16),
            V((HD, EXT), BF16), V((HD, EXT), BF16),
            V((H, EXT, HD), F32), V((H, EXT, HD), F32),
            V((TXT, ROWS), BF16), V((TXT, ROWS), BF16), V((HD, ROWS), BF16),
            V((H, ROWS, HD), BF16), V((H, ROWS, HD), BF16), V((H, ROWS, HD), BF16),
            V((H, 4, FT, HD), BF16), V((H, 4, FT, HD), BF16),
            V((H, NF, 16, HD), BF16), V((H, NX - 1, NZ, 16, HD), BF16), V((H, NZ, 16, HD), BF16),
            V((H, NZ - 1, 16, HD), BF16),
            dma((H, 3, NU)), dma((H, 3, NU)), dma((H, 4)), dma((H, 2, 2)), dma((H, 2, 2)),
            dma((NZ,)), dma((NZ,)), dma((NX,)), dma((NX,)),
            dma((H, 3, NU)), dma((H, 3, NU)), dma((H, 3)), dma((H, 4)), dma((H, 4)),
            dma((H, NZ)), dma((H, NZ)), dma((H, NX)), dma((H, NX)),
        ],
        compiler_params=pltpu.CompilerParams(collective_id=0, has_side_effects=True, vmem_limit_bytes=VMEM_LIMIT),
        name="windowed_attention",
    )(text_len, seg_frames, queries, keys, values, text_k, text_v)


def solution(mesh):
    rows = P(("frame", "uly"), None)
    text = P(None, "frame", "uly")
    return jax.shard_map(
        body,
        mesh=mesh,
        in_specs=(rows, rows, rows, text, text, P(), P()),
        out_specs=(rows, rows, rows, text, text),
        check_vma=False,
    )
```

time: 782 us -> 88.1 us (0.11)
  the two profiles are of different devices: /device:TPU:24 before, /device:TPU:1 now
where the time goes in v2:
time: 88.1 us; the launch traced here: 86.7 us
  Pallas kernels  80.3 us (91%)
  local copies, waits for them, and re-layouts  5.75 us (7%)
    pallas_call x1, Pallas kernels, body(): pl.pallas_call(fused, out_shape=(S((TOK, NU * W), BF16),) * 3 + (S((NSEG,...  80.3 us
    unnamed x13, local copies, waits for them, and re-layouts  5.75 us

profile of v2, /device:TPU:1, one launch (start us, length us, event | category | flops | bytes accessed | tf_op | source)
XLA Modules:
  0.0 86.7 jit_solution(628318002154623008)
XLA Ops:
  0.6 80.3 %windowed_attention.1 = (bf16[128,3072]{1,0:T(8,128)(2,1)}, bf16[128,3072]{1,0:T(8,128)(2,1)}, bf16[128,3072]{1,0:T(8,128)(2,1)}, f32[4,2,384]{2,1,0:T(2,128)}, f32[4,2,384]{2,1,0:T(2,128)}) custom-call(s32[4]{0:T(128)} %lens.1, s32[4]{0:T(128)} %segs.1, bf16[128,3072]{1,0:T(8,128)(2,1)} %q.1, bf16[128,3072]{1,0:T(8,128)(2,1)} %k.1, bf16[128,3072]{1,0:T(8,128)(2,1)} %v.1, ...), custom_call_target="tpu_custom_call" | custom-call | tf_op jit(solution)/shard_map/windowed_attention/pallas_call | solution.py:372
  80.9 0.0 copy-start.1
  80.9 2.1 %copy.17 = bf16[128,3072]{1,0:T(8,128)(2,1)} copy(bf16[128,3072]{1,0:T(8,128)(2,1)} %get-tuple-element.10) | data formatting | bytes 1572864
  83.0 0.0 copy-done.1
  83.0 0.0 copy-start
  83.0 0.9 %copy.18 = bf16[128,3072]{1,0:T(8,128)(2,1)} copy(bf16[128,3072]{1,0:T(8,128)(2,1)S(1)} %copy-done.1) | data formatting | bytes 1572864
  83.9 0.5 copy-done
  84.5 0.0 copy-start.3
  84.5 0.9 %copy.19 = bf16[128,3072]{1,0:T(8,128)(2,1)} copy(bf16[128,3072]{1,0:T(8,128)(2,1)S(1)} %copy-done) | data formatting | bytes 1572864
  85.3 0.0 copy-done.3
  85.3 0.0 copy-start.2
  85.4 0.6 copy.20
  86.0 0.1 copy-done.2
  86.1 0.6 copy.21
Async XLA Ops:
  80.9 2.1 %copy-start.1 = (bf16[128,3072]{1,0:T(8,128)(2,1)S(1)}, bf16[128,3072]{1,0:T(8,128)(2,1)}, u32[]{:S(2)}) copy-start(bf16[128,3072]{1,0:T(8,128)(2,1)} %get-tuple-element.11) | copy-start | bytes 2359300
  83.0 1.4 %copy-start = (bf16[128,3072]{1,0:T(8,128)(2,1)S(1)}, bf16[128,3072]{1,0:T(8,128)(2,1)}, u32[]{:S(2)}) copy-start(bf16[128,3072]{1,0:T(8,128)(2,1)} %get-tuple-element.12) | copy-start | bytes 2359300
  84.5 0.9 %copy-start.3 = (f32[4,2,384]{2,1,0:T(2,128)S(1)}, f32[4,2,384]{2,1,0:T(2,128)}, u32[]{:S(2)}) copy-start(f32[4,2,384]{2,1,0:T(2,128)} %get-tuple-element.13) | copy-start | bytes 36868
  85.3 0.7 copy-start.2

commit v3 on v2

--- a/solution.py
+++ b/solution.py
@@ -23,9 +23,14 @@
 TILES = EXT // TOK
 SCALE = HD ** -0.5
 EXP2 = SCALE * math.log2(math.e)
+QUAD = 4
+FAR = (4, 12, 8)
+NEAR = (1, 15, 2)
 MESH = pl.DeviceIdType.MESH
 VMEM_LIMIT = 56 * 1024 * 1024
 FAR_FIRST = (4, 3, 5, 2, 6, 1, 7)
+GROUPS = (pl.ds(0, 1), pl.ds(1, 2))
+CHUNKS = 4
 BF16 = jnp.bfloat16
 F32 = jnp.float32
 
@@ -36,6 +41,10 @@
     return f, u, lax.div(f, NZ), lax.rem(f, NZ)
 
 
+def slot(z):
+    return lax.rem(z, QUAD) * QUAD + lax.div(z, QUAD)
+
+
 def uly_peer(f, u, d):
     return (f, lax.rem(u + d, NU))
 
@@ -48,15 +57,36 @@
     return (lax.rem(f + NZ * d, NF), u)
 
 
-def meet(f, u, x, z):
+def greet(sem, peer):
+    pl.semaphore_signal(sem, inc=1, device_id=peer, device_id_type=MESH)
+
+
+def each(first, last, act):
+    def one(i, carry):
+        act(i)
+        return carry
+
+    lax.fori_loop(first, last, one, 0)
+
+
+def meet(f, u, x, z, ready):
     barrier = pltpu.get_barrier_semaphore()
-    peers = [uly_peer(f, u, d) for d in range(1, NU)]
-    peers += [z_peer(x, z, u, d) for d in range(1, NZ)]
-    peers += [x_peer(f, u, d) for d in range(1, NX)]
-    peers += [(lax.rem(f + 1, NF), u), (lax.rem(f + NF - 1, NF), u)]
-    for peer in peers:
-        pl.semaphore_signal(barrier, inc=1, device_id=peer, device_id_type=MESH)
-    pl.semaphore_wait(barrier, len(peers))
+    for d in range(1, NU):
+        greet(barrier, uly_peer(f, u, d))
+    each(z + 1, NZ, lambda i: greet(barrier, (x * NZ + i, u)))
+    each(x + 1, NX, lambda i: greet(barrier, (i * NZ + z, u)))
+
+    @pl.when(z == 0)
+    def _():
+        greet(barrier, (lax.rem(f + NF - 1, NF), u))
+
+    pl.semaphore_wait(barrier, NU - 1 + z + x + (z == NZ - 1).astype(jnp.int32))
+    each(0, z, lambda i: greet(ready, (x * NZ + i, u)))
+    each(0, x, lambda i: greet(ready, (i * NZ + z, u)))
+
+    @pl.when(z == NZ - 1)
+    def _():
+        greet(ready, (lax.rem(f + 1, NF), u))
 
 
 def remote(src, dst, send, recv, peer):
@@ -87,15 +117,14 @@
 
 
 def text_in(tg, t32, kv32, tkv, tkvT):
-    for h in range(HEADS):
-        t32[...] = tg[h].reshape(NF * 16, HD).astype(F32)
-        for c in range(2):
-            for s in range(NSEG):
-                for t in range(2):
-                    kv32[c, s, pl.ds(t, NF, stride=2), :] = t32[pl.ds(c * 8 + s * 2 + t, NF, stride=16), :]
-                part = kv32[c, s]
-                tkv[h, c, s] = part.astype(BF16)
-                tkvT[h, c, s] = part.T.astype(BF16)
+    t32[...] = tg[...].reshape(NF * 16, HD).astype(F32)
+    for c in range(2):
+        for s in range(NSEG):
+            for t in range(2):
+                kv32[c, s, pl.ds(t, NF, stride=2), :] = t32[pl.ds(c * 8 + s * 2 + t, NF, stride=16), :]
+            part = kv32[c, s]
+            tkv[c, s] = part.astype(BF16)
+            tkvT[c, s] = part.T.astype(BF16)
 
 
 def turn(src, dst, tiles):
@@ -103,10 +132,16 @@
         dst[:, t * TOK : (t + 1) * TOK] = src[t * TOK : (t + 1) * TOK, :].T
 
 
+def halves(left, c):
+    none = jnp.zeros_like(c)
+    return jnp.concatenate([jnp.where(left, c, none), jnp.where(left, none, c)], axis=0)
+
+
 def pairs_step(pairs, f, lens, bounds, hq, hk, hv, kT, vT, tkv, tkvT, dq, acc_k, acc_v, sc, pc, gT):
     row = lax.broadcasted_iota(jnp.int32, (4 * FT, 2 * FT), 0)
     lane = lax.broadcasted_iota(jnp.int32, (4 * FT, 2 * FT), 1)
-    trow = lax.broadcasted_iota(jnp.int32, (TXT, 2 * FT), 0)
+    place_of = lax.broadcasted_iota(jnp.int32, (TXT, 2 * FT), 0)
+    trow = (place_of & 97) | ((place_of & 6) << 2) | ((place_of & 24) >> 2)
     left = lax.broadcasted_iota(jnp.int32, (TXT, 2 * FT), 1) < FT
     work = []
     for p in pairs:
@@ -132,7 +167,7 @@
     cp16 = [c.astype(BF16) for c in cps]
     so = [dot(vT[:, w[2]], p, 1, 0) for w, p in zip(work, p16)]
     co = [
-        jnp.where(left, dot(tkvT[1, w[3]], c, 1, 0), dot(tkvT[1, w[4]], c, 1, 0)) for w, c in zip(work, cp16)
+        dot(jnp.concatenate([tkvT[1, w[3]], tkvT[1, w[4]]], axis=1), halves(left, c), 1, 0) for w, c in zip(work, cp16)
     ]
     g16 = [(a + b).astype(BF16) for a, b in zip(so, co)]
     sd = [jnp.sum(g.astype(F32) * a, axis=0, keepdims=True) for g, a in zip(g16, so)]
@@ -143,7 +178,10 @@
         for c, w, g, d in zip(cps, work, g16, cd)
     ]
     dqs = [
-        dot(kT[:, w[2]], s, 1, 0) + jnp.where(left, dot(tkvT[0, w[3]], c, 1, 0), dot(tkvT[0, w[4]], c, 1, 0))
+        dot(
+            jnp.concatenate([kT[:, w[2]], tkvT[0, w[3]], tkvT[0, w[4]]], axis=1),
+            jnp.concatenate([s, halves(left, c)], axis=0), 1, 0,
+        )
         for w, s, c in zip(work, ds, dcs)
     ]
     dks = [acc_k[w[2], :] + dot(s, q, 1, 0) for w, s, q in zip(work, ds, qs)]
@@ -162,10 +200,12 @@
     seg = segment(frame, bounds)
     q = hq[...]
     g = gT[...]
+    on = [jnp.broadcast_to((seg == s).astype(F32).astype(BF16)[0:1], (TXT, ROWS)) for s in range(NSEG)]
+    gk = dot(jnp.concatenate([sc[...] * m for m in on], axis=0), q, 1, 0) * SCALE
+    gv = dot(jnp.concatenate([pc[...] * m for m in on], axis=0), g, 1, 1)
     for s in range(NSEG):
-        on = jnp.broadcast_to((seg == s).astype(F32).astype(BF16)[0:1], (TXT, ROWS))
-        kv32[0, s] = dot(sc[...] * on, q, 1, 0) * SCALE
-        kv32[1, s] = dot(pc[...] * on, g, 1, 1)
+        kv32[0, s] = gk[s * TXT : (s + 1) * TXT]
+        kv32[1, s] = gv[s * TXT : (s + 1) * TXT]
     for c in range(2):
         for s in range(NSEG):
             for t in range(2):
@@ -178,7 +218,7 @@
     slab32, slab, hq, hk, hv, tg, t32, kv32, tkv, tkvT, kT, vT, acc_k, acc_v, sc, pc, gT,
     dq, dk, dv, hsend, hrecv, gt, rx, s1, rz,
     a_send, a_recv, l_sem, h_send, h_recv, z_send, z_recv, x_send, x_recv,
-    b_send, b_recv, m_sem, e_send, e_recv, w_send, w_recv, y_send, y_recv,
+    b_send, b_recv, m_sem, e_send, e_recv, w_send, w_recv, y_send, y_recv, ready,
 ):
     f, u, x, z = place()
     bounds = bounds_of(segs)
@@ -189,26 +229,72 @@
         slab32[8 + 2 * s : 8 + 2 * s + 2, :] = tv_in[s].astype(F32)
     for h in range(HEADS):
         slab[h] = slab32[:, h * HD : (h + 1) * HD].astype(BF16)
-    meet(f, u, x, z)
-
-    own_text = pltpu.make_async_copy(slab, tg.at[:, f], l_sem.at[0, 3])
-    zs = [remote(slab, tg.at[:, f], z_send.at[d], z_recv.at[d], z_peer(x, z, u, d)) for d in range(1, NZ)]
+    meet(f, u, x, z, ready)
+
     block = pl.ds(x * NZ, NZ)
-    xs = [
-        remote(tg.at[:, block], tg.at[:, block], x_send.at[d], x_recv.at[d], x_peer(f, u, d)) for d in range(1, NX)
-    ]
-
-    def arrivals(h):
-        local, moves = [], []
-        for i, (src, dst, off) in enumerate(((k, hk, FT), (v, hv, FT), (q, hq, 0))):
-            rows = pl.ds(pl.multiple_of(off + u * TOK, FT), TOK)
-            mine = pl.ds(pl.multiple_of(u * W + h * HD, HD), HD)
-            local.append(pltpu.make_async_copy(src.at[:, mine], dst.at[h, rows], l_sem.at[h, i]))
-            for d in FAR_FIRST:
-                peer = uly_peer(f, u, d)
-                cols = pl.ds(pl.multiple_of(peer[1] * W + h * HD, HD), HD)
-                moves.append(remote(src.at[:, cols], dst.at[h, rows], a_send.at[h, i, d], a_recv.at[h, i, d], peer))
+
+    here = x * NZ + slot(z)
+    row = pl.ds(x * NZ + lax.rem(z, QUAD) * QUAD, QUAD)
+
+    def text_own(g):
+        return pltpu.make_async_copy(slab.at[GROUPS[g]], tg.at[GROUPS[g], here], l_sem.at[g, 3])
+
+    def text_far(g):
+        return [
+            remote(slab.at[GROUPS[g]], tg.at[GROUPS[g], here], z_send.at[g, i], z_recv.at[g, i], z_peer(x, z, u, d))
+            for i, d in enumerate(FAR)
+        ]
+
+    def text_near(g):
+        part = tg.at[GROUPS[g], row]
+        return [
+            remote(part, part, z_send.at[g, 3 + i], z_recv.at[g, 3 + i], z_peer(x, z, u, d)) for i, d in enumerate(NEAR)
+        ]
+
+    def text_over(g):
+        part = tg.at[GROUPS[g], block]
+        return [remote(part, part, x_send.at[g, d], x_recv.at[g, d], x_peer(f, u, d)) for d in range(1, NX)]
+
+    def text_first(g, lower):
+        for c, d in zip(text_far(g), FAR):
+            pl.when((lax.rem(z + d, NZ) < z) == lower)(c.start)
+
+    def text_second(g):
+        text_own(g).wait()
+        for c in text_far(g):
+            c.wait_recv()
+        for c in text_near(g):
+            c.start()
+
+    def text_third(g):
+        for c in text_near(g):
+            c.wait_recv()
+        for c in text_over(g):
+            c.start()
+
+    def arrivals(h, i):
+        src, dst, off = ((k, hk, FT), (v, hv, FT), (q, hq, 0))[i]
+        rows = pl.ds(pl.multiple_of(off + u * TOK, FT), TOK)
+        mine = pl.ds(pl.multiple_of(u * W + h * HD, HD), HD)
+        local = pltpu.make_async_copy(src.at[:, mine], dst.at[h, rows], l_sem.at[h, i])
+        moves = []
+        for d in FAR_FIRST:
+            peer = uly_peer(f, u, d)
+            cols = pl.ds(pl.multiple_of(peer[1] * W + h * HD, HD), HD)
+            moves.append(remote(src.at[:, cols], dst.at[h, rows], a_send.at[h, i, d], a_recv.at[h, i, d], peer))
         return local, moves
+
+    def issue(h, i):
+        local, moves = arrivals(h, i)
+        local.start()
+        for c in moves:
+            c.start()
+
+    def landed(h, i):
+        local, moves = arrivals(h, i)
+        local.wait()
+        for c in moves:
+            c.wait_recv()
 
     def halo_in(h):
         out = []
@@ -248,22 +334,23 @@
 
     def text_z(h):
         return [
-            remote(s1.at[h, lax.rem(z + d, NZ)], rz.at[h, d - 1], w_send.at[h, d], w_recv.at[h, d], z_peer(x, z, u, d))
+            remote(s1.at[h, slot(lax.rem(z + d, NZ))], rz.at[h, d - 1], w_send.at[h, d], w_recv.at[h, d], z_peer(x, z, u, d))
             for d in range(1, NZ)
         ]
 
-    def finish_edges(h):
+    def give(h, i):
+        local, moves = returns(h, i)
+        local.start()
+        for c in moves:
+            c.start()
+
+    def add_edges(h):
         for c in halo_out(h):
             c.wait_recv()
         for i, (acc, out) in enumerate(((acc_k, dk), (acc_v, dv))):
             scale = SCALE if i == 0 else 1.0
             out[h, 0:FT] = (acc[h, FT : 2 * FT] * scale + hrecv[h, 2 * i].astype(F32)).astype(BF16)
             out[h, ROWS - FT : ROWS] = (acc[h, ROWS : ROWS + FT] * scale + hrecv[h, 2 * i + 1].astype(F32)).astype(BF16)
-        for i in (1, 2):
-            local, moves = returns(h, i)
-            local.start()
-            for c in moves:
-                c.start()
 
     def text_mid(h):
         for c in text_x(h):
@@ -275,36 +362,37 @@
         for c in text_z(h):
             c.start()
 
-    for c in zs:
-        c.start()
-    own_text.start()
+    for g in range(2):
+        text_own(g).start()
+        text_first(g, True)
     for h in range(HEADS):
-        local, moves = arrivals(h)
-        for c in local + moves:
-            c.start()
+        for i in range(3):
+            issue(h, i)
+    later = NZ - 1 - z + NX - 1 - x + (z == 0).astype(jnp.int32)
+
+    @pl.when(later > 0)
+    def _():
+        pl.semaphore_wait(ready, later)
+
+    for g in range(2):
+        text_first(g, False)
     acc_k[...] = jnp.zeros_like(acc_k)
     acc_v[...] = jnp.zeros_like(acc_v)
-    own_text.wait()
-    for c in zs:
-        c.wait_recv()
-    for c in xs:
-        c.start()
-
-    for h in range(HEADS):
-        local, moves = arrivals(h)
-        for c in local:
-            c.wait()
-        for c in moves:
-            c.wait_recv()
-        halo = halo_in(h)
-        for c in halo:
-            c.start()
+
+    def halo_start(h):
+        landed(h, 0)
+        landed(h, 1)
+        for c in halo_in(h):
+            c.start()
+
+    def compute(h):
         turn(hk.at[h], kT, range(1, TILES - 1))
         turn(hv.at[h], vT, range(1, TILES - 1))
-        if h == 0:
-            for c in xs:
+        if h < 2:
+            for c in text_over(h):
                 c.wait_recv()
-            text_in(tg, t32, kv32, tkv, tkvT)
+        text_in(tg.at[h], t32, kv32, tkv.at[h], tkvT.at[h])
+        landed(h, 2)
         refs = (
             f, lens, bounds, hq.at[h], hk.at[h], hv.at[h], kT, vT, tkv.at[h], tkvT.at[h], dq.at[h],
             acc_k.at[h], acc_v.at[h], sc, pc, gT,
@@ -315,50 +403,105 @@
             return carry
 
         lax.fori_loop(0, 3, inner, 0)
-        for c in halo:
+        for c in halo_in(h):
             c.wait_recv()
         turn(hk.at[h], kT, (0, TILES - 1))
         turn(hv.at[h], vT, (0, TILES - 1))
         pairs_step((0, 7), *refs)
+
+    def halo_back(h):
         for i, acc in enumerate((acc_k, acc_v)):
             scale = SCALE if i == 0 else 1.0
             hsend[h, 2 * i] = (acc[h, 0:FT] * scale).astype(BF16)
             hsend[h, 2 * i + 1] = (acc[h, FT + ROWS : EXT] * scale).astype(BF16)
         for c in halo_out(h):
             c.start()
-        local, moves = returns(h, 0)
-        local.start()
-        for c in moves:
-            c.start()
+
+    def text_sum(h):
         text_out(f, bounds, hq.at[h], sc, pc, gT, t32, kv32, gt.at[h])
         for c in text_x(h):
             c.start()
+
+    def round_own(h):
         dk[h, FT : ROWS - FT] = (acc_k[h, 2 * FT : ROWS] * SCALE).astype(BF16)
         dv[h, FT : ROWS - FT] = acc_v[h, 2 * FT : ROWS].astype(BF16)
-        finish_edges(h)
-        if h > 0:
-            text_mid(h - 1)
-    text_mid(HEADS - 1)
+
+    text_second(0)
+    text_second(1)
+    text_third(0)
+    halo_start(0)
+    text_third(1)
+    halo_start(1)
+    compute(0)
+    halo_start(2)
+    halo_back(0)
+    give(0, 0)
+    text_sum(0)
+    round_own(0)
+    add_edges(0)
+    give(0, 1)
+    give(0, 2)
+    compute(1)
+    halo_back(1)
+    give(1, 0)
+    text_sum(1)
+    round_own(1)
+    text_mid(0)
+    add_edges(1)
+    give(1, 1)
+    give(1, 2)
+    compute(2)
+    halo_back(2)
+    text_sum(2)
+    give(2, 0)
+    text_mid(1)
+    round_own(2)
+    add_edges(2)
+    text_mid(2)
+    give(2, 1)
+    give(2, 2)
     for h in range(HEADS):
         for c in text_z(h):
             c.wait_recv()
-        last = s1[h, z].astype(F32)
+        last = s1[h, slot(z)].astype(F32)
         for d in range(1, NZ):
             last = last + rz[h, d - 1].astype(F32)
         cols = slice(h * HD, (h + 1) * HD)
         for s in range(NSEG):
             ogk[s, :, cols] = last[2 * s : 2 * s + 2]
             ogv[s, :, cols] = last[8 + 2 * s : 8 + 2 * s + 2]
-    for c in zs + xs:
-        c.wait_send()
+    for g in range(2):
+        for c in text_far(g) + text_near(g) + text_over(g):
+            c.wait_send()
     for h in range(HEADS):
-        for c in arrivals(h)[1] + halo_in(h) + halo_out(h) + text_x(h) + text_z(h):
+        for c in halo_in(h) + halo_out(h) + text_x(h) + text_z(h):
             c.wait_send()
         for i in range(3):
+            for c in arrivals(h, i)[1]:
+                c.wait_send()
             local, moves = returns(h, i)
             local.wait()
             for c in moves:
                 c.wait()
+
+
+def deliver(a, b, c, d, e, oa, ob, oc, od, oe, buf, come, go):
+    rows = TOK // CHUNKS
+    ins, outs = [], []
+    for i, (src, dst) in enumerate(((a, oa), (b, ob), (c, oc))):
+        for j in range(CHUNKS):
+            part = pl.ds(j * rows, rows)
+            ins.append(pltpu.make_async_copy(src.at[part], buf.at[i, part], come.at[i, j]))
+            outs.append(pltpu.make_async_copy(buf.at[i, part], dst.at[part], go.at[i, j]))
+    for m in ins:
+        m.start()
+    od[...] = d[...]
+    oe[...] = e[...]
+    for m, n in zip(ins, outs):
+        m.wait()
+        n.start()
+    for n in outs:
+        n.wait()
 
 
 def body(queries, keys, values, text_k, text_v, text_len, seg_frames):
@@ -369,9 +512,10 @@
     S = jax.ShapeDtypeStruct
     V = pltpu.VMEM
     H = HEADS
-    return pl.pallas_call(
+    shapes = (S((TOK, NU * W), BF16),) * 3 + (S((NSEG, 2, W), F32),) * 2
+    grads = pl.pallas_call(
         fused,
-        out_shape=(S((TOK, NU * W), BF16),) * 3 + (S((NSEG, 2, W), F32),) * 2,
+        out_shape=shapes,
         in_specs=[smem, smem, hbm, hbm, hbm, vmem, vmem],
         out_specs=(hbm, hbm, hbm, vmem, vmem),
         scratch_shapes=[
@@ -387,13 +531,22 @@
             V((H, NF, 16, HD), BF16), V((H, NX - 1, NZ, 16, HD), BF16), V((H, NZ, 16, HD), BF16),
             V((H, NZ - 1, 16, HD), BF16),
             dma((H, 3, NU)), dma((H, 3, NU)), dma((H, 4)), dma((H, 2, 2)), dma((H, 2, 2)),
-            dma((NZ,)), dma((NZ,)), dma((NX,)), dma((NX,)),
+            dma((2, 6)), dma((2, 6)), dma((2, NX)), dma((2, NX)),
             dma((H, 3, NU)), dma((H, 3, NU)), dma((H, 3)), dma((H, 4)), dma((H, 4)),
             dma((H, NZ)), dma((H, NZ)), dma((H, NX)), dma((H, NX)),
+            pltpu.SemaphoreType.REGULAR,
         ],
         compiler_params=pltpu.CompilerParams(collective_id=0, has_side_effects=True, vmem_limit_bytes=VMEM_LIMIT),
         name="windowed_attention",
     )(text_len, seg_frames, queries, keys, values, text_k, text_v)
+    return pl.pallas_call(
+        deliver,
+        out_shape=shapes,
+        in_specs=[hbm, hbm, hbm, vmem, vmem],
+        out_specs=(hbm, hbm, hbm, vmem, vmem),
+        scratch_shapes=[V((3, TOK, NU * W), BF16), dma((3, CHUNKS)), dma((3, CHUNKS))],
+        name="deliver",
+    )(*grads)
 
 
 def solution(mesh):

time: 88.1 us -> 84.4 us (0.958); the launches traced: 86.7 us -> 84.1 us
  local copies, waits for them, and re-layouts: 5.75 us -> 0 us
  Pallas kernels: 80.3 us -> 83.5 us
    unnamed x13 -> x0, local copies, waits for them, and re-layouts: 5.75 us -> none
    pallas_call x1 -> x2, Pallas kernels: 80.3 us -> 83.5 us  [the longest x1 79.5 us: body(): pl.pallas_call(fused, out_shape=shapes, in_specs=[smem, smem, hbm, hbm, h...]
where the time goes in v3:
time: 84.4 us; the launch traced here: 84.1 us
  Pallas kernels  83.5 us (99%)
    pallas_call x1, Pallas kernels, body(): pl.pallas_call(fused, out_shape=shapes, in_specs=[smem, smem, hbm, hbm, h...  79.5 us
    pallas_call x1, Pallas kernels, body(): pl.pallas_call(deliver, out_shape=shapes, in_specs=[hbm, hbm, hbm, vmem,...  3.95 us

profile of v3, /device:TPU:1, one launch (start us, length us, event | category | flops | bytes accessed | tf_op | source)
XLA Modules:
  0.0 84.1 jit_solution(2381765531812809276)
XLA Ops:
  0.6 79.5 %windowed_attention.1 = (bf16[128,3072]{1,0:T(8,128)(2,1)}, bf16[128,3072]{1,0:T(8,128)(2,1)}, bf16[128,3072]{1,0:T(8,128)(2,1)}, f32[4,2,384]{2,1,0:T(2,128)}, f32[4,2,384]{2,1,0:T(2,128)}) custom-call(s32[4]{0:T(128)} %lens.1, s32[4]{0:T(128)} %segs.1, bf16[128,3072]{1,0:T(8,128)(2,1)} %q.1, bf16[128,3072]{1,0:T(8,128)(2,1)} %k.1, bf16[128,3072]{1,0:T(8,128)(2,1)} %v.1, ...), custom_call_target="tpu_custom_call" | custom-call | tf_op jit(solution)/shard_map/windowed_attention/pallas_call | solution.py:516
  80.2 4.0 %deliver.1 = (bf16[128,3072]{1,0:T(8,128)(2,1)}, bf16[128,3072]{1,0:T(8,128)(2,1)}, bf16[128,3072]{1,0:T(8,128)(2,1)}, f32[4,2,384]{2,1,0:T(2,128)}, f32[4,2,384]{2,1,0:T(2,128)}) custom-call(bf16[128,3072]{1,0:T(8,128)(2,1)} %get-tuple-element.10.a, bf16[128,3072]{1,0:T(8,128)(2,1)} %get-tuple-element.11.b, bf16[128,3072]{1,0:T(8,128)(2,1)} %get-tuple-element.12.c, ...), custom_call_target="tpu_custom_call" | custom-call | tf_op jit(solution)/shard_map/deliver/pallas_call | solution.py:542

commit v4 on v3

--- a/solution.py
+++ b/solution.py
@@ -30,7 +30,7 @@
 VMEM_LIMIT = 56 * 1024 * 1024
 FAR_FIRST = (4, 3, 5, 2, 6, 1, 7)
 GROUPS = (pl.ds(0, 1), pl.ds(1, 2))
-CHUNKS = 4
+CHUNKS = 2
 BF16 = jnp.bfloat16
 F32 = jnp.float32
 
@@ -485,18 +485,19 @@
                 c.wait()
 
 
-def deliver(a, b, c, d, e, oa, ob, oc, od, oe, buf, come, go):
+def deliver(a, b, c, d, e, oa, ob, oc, od, oe, buf, tbuf, come, go):
     rows = TOK // CHUNKS
     ins, outs = [], []
-    for i, (src, dst) in enumerate(((a, oa), (b, ob), (c, oc))):
-        for j in range(CHUNKS):
+    for j in range(CHUNKS):
+        for i, (src, dst) in enumerate(((a, oa), (b, ob), (c, oc))):
             part = pl.ds(j * rows, rows)
             ins.append(pltpu.make_async_copy(src.at[part], buf.at[i, part], come.at[i, j]))
             outs.append(pltpu.make_async_copy(buf.at[i, part], dst.at[part], go.at[i, j]))
+    for i, (src, dst) in enumerate(((d, od), (e, oe))):
+        ins.append(pltpu.make_async_copy(src, tbuf.at[i], come.at[3, i]))
+        outs.append(pltpu.make_async_copy(tbuf.at[i], dst, go.at[3, i]))
     for m in ins:
         m.start()
-    od[...] = d[...]
-    oe[...] = e[...]
     for m, n in zip(ins, outs):
         m.wait()
         n.start()
@@ -542,9 +543,10 @@
     return pl.pallas_call(
         deliver,
         out_shape=shapes,
-        in_specs=[hbm, hbm, hbm, vmem, vmem],
-        out_specs=(hbm, hbm, hbm, vmem, vmem),
-        scratch_shapes=[V((3, TOK, NU * W), BF16), dma((3, CHUNKS)), dma((3, CHUNKS))],
+        in_specs=[hbm] * 5,
+        out_specs=(hbm,) * 5,
+        scratch_shapes=[V((3, TOK, NU * W), BF16), V((2, NSEG, 2, W), F32), dma((4, CHUNKS)), dma((4, CHUNKS))],
+        compiler_params=pltpu.CompilerParams(vmem_limit_bytes=8 * 1024 * 1024),
         name="deliver",
     )(*grads)
 

time: 84.4 us -> 88 us (1.043)
  local copies, waits for them, and re-layouts: 0 us -> 4.8 us
  Pallas kernels: 83.5 us -> 82.2 us
    unnamed x0 -> x10, local copies, waits for them, and re-layouts: none -> 4.8 us
    pallas_call x1, Pallas kernels: 3.95 us -> 2.68 us  [body(): pl.pallas_call(deliver, out_shape=shapes, in_specs=[hbm] * 5, out_specs=(...]
where the time goes in v4:
time: 88 us; the launch traced here: 87.6 us
  Pallas kernels  82.2 us (93%)
  local copies, waits for them, and re-layouts  4.8 us (5%)
    pallas_call x1, Pallas kernels, body(): pl.pallas_call(fused, out_shape=shapes, in_specs=[smem, smem, hbm, hbm, h...  79.5 us
    unnamed x10, local copies, waits for them, and re-layouts  4.8 us
    pallas_call x1, Pallas kernels, body(): pl.pallas_call(deliver, out_shape=shapes, in_specs=[hbm] * 5, out_specs=(...  2.68 us

profile of v4, /device:TPU:1, one launch (start us, length us, event | category | flops | bytes accessed | tf_op | source)
XLA Modules:
  0.0 87.6 jit_solution(8841327733253407784)
XLA Ops:
  0.6 79.5 %windowed_attention.1 = (bf16[128,3072]{1,0:T(8,128)(2,1)}, bf16[128,3072]{1,0:T(8,128)(2,1)}, bf16[128,3072]{1,0:T(8,128)(2,1)}, f32[4,2,384]{2,1,0:T(2,128)}, f32[4,2,384]{2,1,0:T(2,128)}) custom-call(s32[4]{0:T(128)} %lens.1, s32[4]{0:T(128)} %segs.1, bf16[128,3072]{1,0:T(8,128)(2,1)} %q.1, bf16[128,3072]{1,0:T(8,128)(2,1)} %k.1, bf16[128,3072]{1,0:T(8,128)(2,1)} %v.1, ...), custom_call_target="tpu_custom_call" | custom-call | tf_op jit(solution)/shard_map/windowed_attention/pallas_call | solution.py:517
  80.2 0.0 copy-start
  80.2 1.1 %copy-done = bf16[128,3072]{1,0:T(8,128)(2,1)S(1)} copy-done((bf16[128,3072]{1,0:T(8,128)(2,1)S(1)}, bf16[128,3072]{1,0:T(8,128)(2,1)}, u32[]{:S(2)}) %copy-start) | copy-done | bytes 786456
  81.3 0.0 copy-start.1
  81.3 1.1 %copy-done.1 = bf16[128,3072]{1,0:T(8,128)(2,1)S(1)} copy-done((bf16[128,3072]{1,0:T(8,128)(2,1)S(1)}, bf16[128,3072]{1,0:T(8,128)(2,1)}, u32[]{:S(2)}) %copy-start.1) | copy-done | bytes 786456
  82.4 0.0 copy-start.2
  82.4 1.1 %copy-done.2 = bf16[128,3072]{1,0:T(8,128)(2,1)S(1)} copy-done((bf16[128,3072]{1,0:T(8,128)(2,1)S(1)}, bf16[128,3072]{1,0:T(8,128)(2,1)}, u32[]{:S(2)}) %copy-start.2) | copy-done | bytes 786456
  83.6 0.0 copy-start.3
  83.6 0.7 copy-done.3
  84.3 0.0 copy-start.4
  84.3 0.7 copy-done.4
  85.0 2.7 %deliver.1 = (bf16[128,3072]{1,0:T(8,128)(2,1)}, bf16[128,3072]{1,0:T(8,128)(2,1)}, bf16[128,3072]{1,0:T(8,128)(2,1)}, f32[4,2,384]{2,1,0:T(2,128)}, f32[4,2,384]{2,1,0:T(2,128)}) custom-call(bf16[128,3072]{1,0:T(8,128)(2,1)S(1)} %copy-done, bf16[128,3072]{1,0:T(8,128)(2,1)S(1)} %copy-done.1, bf16[128,3072]{1,0:T(8,128)(2,1)S(1)} %copy-done.2, ...), custom_call_target="tpu_custom_call" | custom-call | tf_op jit(solution)/shard_map/deliver/pallas_call | solution.py:543
Async XLA Ops:
  80.2 1.1 %copy-start = (bf16[128,3072]{1,0:T(8,128)(2,1)S(1)}, bf16[128,3072]{1,0:T(8,128)(2,1)}, u32[]{:S(2)}) copy-start(bf16[128,3072]{1,0:T(8,128)(2,1)} %get-tuple-element.10.a) | copy-start | bytes 2359300
  81.3 1.1 %copy-start.1 = (bf16[128,3072]{1,0:T(8,128)(2,1)S(1)}, bf16[128,3072]{1,0:T(8,128)(2,1)}, u32[]{:S(2)}) copy-start(bf16[128,3072]{1,0:T(8,128)(2,1)} %get-tuple-element.11.b) | copy-start | bytes 2359300
  82.4 1.1 %copy-start.2 = (bf16[128,3072]{1,0:T(8,128)(2,1)S(1)}, bf16[128,3072]{1,0:T(8,128)(2,1)}, u32[]{:S(2)}) copy-start(bf16[128,3072]{1,0:T(8,128)(2,1)} %get-tuple-element.12.c) | copy-start | bytes 2359300
  83.6 0.7 copy-start.3
  84.3 0.7 copy-start.4
